TPU v7x, 256 devices: a whole 4x4x8 slice. The times are simulated.
256 devices in a mesh: row: 16 (over x, y_lo, core), col: 16 (over y_hi, z).
Axes of the slice: x: 4, y: 4 (y_hi: 2, y_lo: 2; y = y_hi * 2 + y_lo), z: 8, core: 2. Of those that a mesh axis runs over, the one named last changes fastest.
Arguments:
- queries: bfloat16 [1024, 192], P(('row', 'col')), may hold values from -12 to 12
- query_points: bfloat16 [1024, 144], P(('row', 'col')), may hold values from -4 to 4
- key_feats: bfloat16 [1024, 192], P(('col', 'row')), may hold values from -12 to 12
- key_points: bfloat16 [1024, 144], P(('col', 'row')), may hold values from -4 to 4
- values: bfloat16 [1024, 192], P(('col', 'row')), may hold values from -5 to 5
- value_points: bfloat16 [1024, 288], P(('col', 'row')), may hold values from -5 to 5
- pair_rep: float32 [1024, 1024, 128], P('row', 'col'), may hold values from -6 to 6
- bias_weight: float32 [128, 12], replicated, may hold values from -0.5 to 0.5
- head_weight: float32 [12], replicated, may hold values from 0.1 to 1
- chain_bias: float32 [12], replicated, may hold values from -3 to 3
- chain_ids: int32 [1024], replicated, may hold values from 0 to 7, never falling along the last dimension, each value on 1 to 256 neighbouring positions
- live_mask: int32 [1024], replicated, may hold values from 0 to 1, as said below
- cot_scalar: bfloat16 [1024, 192], P(('row', 'col')), may hold values from -5 to 5
- cot_points: bfloat16 [1024, 288], P(('row', 'col')), may hold values from -5 to 5
- cot_pair: bfloat16 [1024, 1536], P(('row', 'col')), may hold values from -5 to 5
Outputs:
- grad_queries: float32 [1024, 192], P(('row', 'col'))
- grad_query_points: float32 [1024, 144], P(('row', 'col'))
- grad_keys: float32 [1024, 192], P(('col', 'row'))
- grad_key_points: float32 [1024, 144], P(('col', 'row'))
- grad_values: float32 [1024, 192], P(('col', 'row'))
- grad_value_points: float32 [1024, 288], P(('col', 'row'))
- grad_pair: float32 [1024, 1024, 128], P('row', 'col')
- grad_bias_weight: float32 [128, 12], replicated
Inputs may be any that keep to these rules, and one draw needn't show every extreme that they name: `live_mask`: at least one residue is live.
All inputs are finite; a program needn't handle non-finite values.
Results may differ from a plain program's by a relative error of at most 0.0175.
Values may be sent and summed in bfloat16 or wider, within the bound.
A program may use at most 64 MiB of HBM per device.

v0:
```python
import math

import jax
import jax.numpy as jnp
from jax import lax
from jax.sharding import PartitionSpec as P

HIGH = lax.Precision.HIGHEST
NEG_FILL = -1e30


def merged(value, axis, join):
    pieces = jax.tree.map(lambda part: lax.all_gather(part, axis), value)
    head = jax.tree.map(lambda part: part[0], pieces)
    tail = jax.tree.map(lambda part: part[1:], pieces)
    running, _ = lax.scan(lambda running, piece: (join(running, piece), None), head, tail)
    return running


def combine_pair(earlier, later):
    row_max = jnp.maximum(earlier[0], later[0])
    return (
        row_max,
        earlier[1] * jnp.exp(earlier[0] - row_max) + later[1] * jnp.exp(later[0] - row_max),
    )


def key_side_sums(ds_part, pr_part, kp_part, q3, qp3, gsc3, gpt3, kp_scale, scale_q):
    row_count = ds_part.shape[2]
    grad_k = scale_q * jnp.einsum("hij,ihc->jhc", ds_part, q3, preferred_element_type=jnp.float32)
    col_sums = jnp.sum(ds_part.astype(jnp.float32), 1).T
    grad_kp = (
        -2.0
        * kp_scale[None, :, None]
        * (
            col_sums[:, :, None] * kp_part
            - jnp.einsum("hij,ihd->jhd", ds_part, qp3, preferred_element_type=jnp.float32)
        )
    )
    grad_v = jnp.einsum("hij,ihc->jhc", pr_part, gsc3, preferred_element_type=jnp.float32)
    grad_vp = jnp.einsum("hij,ihd->jhd", pr_part, gpt3, preferred_element_type=jnp.float32)
    return jnp.concatenate(
        (
            grad_k.reshape(row_count, -1),
            grad_kp.reshape(row_count, -1),
            grad_v.reshape(row_count, -1),
            grad_vp.reshape(row_count, -1),
        ),
        1,
    )


def on_device(
    queries,
    query_points,
    key_feats,
    key_points,
    values,
    value_points,
    pair_rep,
    bias_weight,
    head_weight,
    chain_bias,
    chain_ids,
    live_mask,
    cot_scalar,
    cot_points,
    cot_pair,
):
    num_heads = head_weight.shape[0]
    head_size = queries.shape[1] // num_heads
    channels = bias_weight.shape[0]
    tile_rows = pair_rep.shape[0]
    tile_cols = pair_rep.shape[1]
    npoint_q = query_points.shape[1] // (3 * num_heads)
    w_logit = math.sqrt(1.0 / 3.0)
    w_point = math.sqrt(2.0 / (9.0 * npoint_q))
    point_scale = w_logit * head_weight * w_point / 2.0
    scale_q = w_logit / math.sqrt(head_size)
    row_start = lax.axis_index("row") * tile_rows
    col_start = lax.axis_index("col") * tile_cols
    chain_q = lax.dynamic_slice_in_dim(chain_ids, row_start, tile_rows)
    chain_k = lax.dynamic_slice_in_dim(chain_ids, col_start, tile_cols)
    live_q = lax.dynamic_slice_in_dim(live_mask, row_start, tile_rows).astype(jnp.bfloat16)
    live_k = lax.dynamic_slice_in_dim(live_mask, col_start, tile_cols).astype(jnp.float32)
    key_all, kpt_all, val_all, vpt_all = (
        lax.all_gather(key_feats, "row", axis=0, tiled=True),
        lax.all_gather(key_points, "row", axis=0, tiled=True),
        lax.all_gather(values, "row", axis=0, tiled=True),
        lax.all_gather(value_points, "row", axis=0, tiled=True),
    )
    q_all, qpt_all, gsc_all, gpt_all, gpr_all = (
        lax.all_gather(queries, "col", axis=0, tiled=True),
        lax.all_gather(query_points, "col", axis=0, tiled=True),
        lax.all_gather(cot_scalar, "col", axis=0, tiled=True),
        lax.all_gather(cot_points, "col", axis=0, tiled=True),
        lax.all_gather(cot_pair, "col", axis=0, tiled=True),
    )
    early = (gsc_all, gpt_all, gpr_all)
    q3 = q_all.reshape(tile_rows, num_heads, head_size)
    qp3 = qpt_all.reshape(tile_rows, num_heads, -1)
    k3 = key_all.reshape(tile_cols, num_heads, head_size)
    kp3 = kpt_all.reshape(tile_cols, num_heads, -1)
    v3 = val_all.reshape(tile_cols, num_heads, head_size)
    vp3 = vpt_all.reshape(tile_cols, num_heads, -1)
    qp_f = qp3.astype(jnp.float32)
    kp_f = kp3.astype(jnp.float32)
    q_sq = jnp.sum(qp_f * qp_f, -1).T
    k_sq = jnp.sum(kp_f * kp_f, -1).T
    scalar_dot = jnp.einsum("ihc,jhc->hij", q3, k3, preferred_element_type=jnp.float32)
    point_dot = jnp.einsum("ihd,jhd->hij", qp3, kp3, preferred_element_type=jnp.float32)
    distance = q_sq[:, :, None] + k_sq[:, None, :] - 2.0 * point_dot
    pair_bias = jnp.einsum("ijc,ch->hij", pair_rep, bias_weight, precision=HIGH)
    same_chain = (chain_q[:, None] == chain_k[None, :]).astype(jnp.float32)
    logits = (
        w_logit
        * (scalar_dot / math.sqrt(head_size) + pair_bias + chain_bias[:, None, None] * same_chain)
        - point_scale[:, None, None] * distance
    )
    logits = jnp.where(live_k[None, None, :] > 0, logits, NEG_FILL)
    local_max = jnp.max(logits, -1)
    local_exp = jnp.exp(logits - local_max[:, :, None]) * live_k[None, None, :]
    row_max, row_total = merged((local_max, jnp.sum(local_exp, -1)), "col", combine_pair)
    cot_sc, cot_pt, cot_pr = tuple((member * live_q[:, None] for member in early))
    gsc3 = cot_sc.reshape(tile_rows, num_heads, head_size)
    gpt3 = cot_pt.reshape(tile_rows, num_heads, -1)
    gpr3 = cot_pr.reshape(tile_rows, num_heads, channels)
    prob = jnp.exp(logits - row_max[:, :, None]) * live_k[None, None, :] / row_total[:, :, None]
    dprob = jnp.einsum("ihc,jhc->hij", gsc3, v3, preferred_element_type=jnp.float32)
    dprob = dprob + jnp.einsum("ihd,jhd->hij", gpt3, vp3, preferred_element_type=jnp.float32)
    dprob = dprob + jnp.einsum("ihc,ijc->hij", gpr3.astype(jnp.float32), pair_rep, precision=HIGH)
    dsum = lax.psum(jnp.sum(prob * dprob, -1), "col")
    dscore = prob * (dprob - dsum[:, :, None])
    prob16 = prob.astype(jnp.bfloat16)
    ds16 = dscore.astype(jnp.bfloat16)
    grad_pair = jnp.einsum("hij,ihc->ijc", prob16, gpr3, preferred_element_type=jnp.float32)
    grad_pair = grad_pair + w_logit * jnp.einsum("hij,ch->ijc", dscore, bias_weight, precision=HIGH)
    weight_term = w_logit * jnp.einsum("ijc,hij->ch", pair_rep, dscore, precision=HIGH)
    grad_bias_weight = lax.psum(weight_term, ("row", "col"))
    ds_part = ds16
    grad_q = scale_q * jnp.einsum("hij,jhc->ihc", ds_part, k3, preferred_element_type=jnp.float32)
    row_sums = jnp.sum(ds_part.astype(jnp.float32), -1).T
    grad_qp = (
        -2.0
        * point_scale[None, :, None]
        * (
            row_sums[:, :, None] * qp_f
            - jnp.einsum("hij,jhd->ihd", ds_part, kp3, preferred_element_type=jnp.float32)
        )
    )
    query_side = lax.psum_scatter(
        jnp.concatenate(
            (
                grad_q.reshape(lax.axis_size("col") * (tile_rows // lax.axis_size("col")), -1),
                grad_qp.reshape(lax.axis_size("col") * (tile_rows // lax.axis_size("col")), -1),
            ),
            1,
        ),
        "col",
        scatter_dimension=0,
        tiled=True,
    )
    ds_part = ds16
    key_side = lax.psum_scatter(
        key_side_sums(ds_part, prob16, kp_f, q3, qp3, gsc3, gpt3, point_scale, scale_q),
        "row",
        scatter_dimension=0,
        tiled=True,
    )
    width_s = num_heads * head_size
    width_q = query_points.shape[1]
    width_v = value_points.shape[1]
    grad_queries = query_side[:, :width_s]
    grad_query_points = query_side[:, width_s:]
    grad_keys = key_side[:, :width_s]
    grad_key_points = key_side[:, width_s : width_s + width_q]
    grad_values = key_side[:, width_s + width_q : 2 * width_s + width_q]
    grad_value_points = key_side[:, 2 * width_s + width_q : 2 * width_s + width_q + width_v]
    return (
        grad_queries,
        grad_query_points,
        grad_keys,
        grad_key_points,
        grad_values,
        grad_value_points,
        grad_pair,
        grad_bias_weight,
    )


def solution(mesh):
    return jax.shard_map(
        on_device,
        mesh=mesh,
        in_specs=(
            P(("row", "col"), None),
            P(("row", "col"), None),
            P(("col", "row"), None),
            P(("col", "row"), None),
            P(("col", "row"), None),
            P(("col", "row"), None),
            P("row", "col", None),
            P(),
            P(),
            P(),
            P(),
            P(),
            P(("row", "col"), None),
            P(("row", "col"), None),
            P(("row", "col"), None),
        ),
        out_specs=(
            P(("row", "col"), None),
            P(("row", "col"), None),
            P(("col", "row"), None),
            P(("col", "row"), None),
            P(("col", "row"), None),
            P(("col", "row"), None),
            P("row", "col", None),
            P(),
        ),
        check_vma=False,
    )
```

profile of v0, /device:TPU:1, one launch (start us, length us, event | category | flops | bytes accessed | tf_op | source)
XLA Modules:
  0.0 678.1 jit_solution(6013700597097572778)
XLA Ops:
  7.3 1.5 copy-done
  8.8 5.7 fusion.22
  14.5 0.2 copy.81
  14.7 37.8 %all-gather.2 = bf16[16,4,192]{2,1,0:T(4,128)(2,1)S(1)} all-gather(bf16[1,4,192]{2,1,0:T(4,128)(2,1)S(1)} %bitcast.123), channel_id=1, replica_groups=mesh['row'=16,'col'=16] {'col'}, dimensions={0}, use_global_device_ids=true | all-gather | bytes 26112 | tf_op jit(solution)/shard_map/all_gather | solution.py:93
  52.5 0.2 reshape.105
  52.7 0.2 copy.79
  52.9 26.6 %all-gather.3 = bf16[16,4,192]{2,1,0:T(4,128)(2,1)S(1)} all-gather(bf16[1,4,192]{2,1,0:T(4,128)(2,1)S(1)} %bitcast.124), channel_id=1, replica_groups=mesh['row'=16,'col'=16] {'row'}, dimensions={0}, use_global_device_ids=true | all-gather | bytes 26112 | tf_op jit(solution)/shard_map/all_gather | solution.py:87
  79.5 0.2 reshape.106
  79.7 0.2 copy.80
  80.0 28.8 %all-gather.4 = bf16[16,4,144]{2,1,0:T(4,128)(2,1)S(1)} all-gather(bf16[1,4,144]{2,1,0:T(4,128)(2,1)S(1)} %bitcast.125), channel_id=1, replica_groups=mesh['row'=16,'col'=16] {'col'}, dimensions={0}, use_global_device_ids=true | all-gather | bytes 19584 | tf_op jit(solution)/shard_map/all_gather | solution.py:94
  108.8 0.3 reshape.107
  109.1 0.3 copy.82
  109.3 23.3 %all-gather.5 = bf16[16,4,144]{2,1,0:T(4,128)(2,1)S(1)} all-gather(bf16[1,4,144]{2,1,0:T(4,128)(2,1)S(1)} %bitcast.126), channel_id=1, replica_groups=mesh['row'=16,'col'=16] {'row'}, dimensions={0}, use_global_device_ids=true | all-gather | bytes 19584 | tf_op jit(solution)/shard_map/all_gather | solution.py:88
  132.6 0.3 reshape.108
  132.9 0.3 copy.83
  133.2 0.5 broadcast_multiply_fusion.3
  133.8 0.8 broadcast_compare_fusion
  134.5 0.8 fusion.26
  135.4 0.3 fusion.9
  135.7 0.3 fusion.27
  136.1 30.9 %all-gather.6 = f32[16,12,64]{2,1,0:T(8,128)S(1)} all-gather(f32[1,12,64]{2,1,0:T(8,128)S(1)} %bitcast.114), channel_id=2, replica_groups=mesh['row'=16,'col'=16] {'col'}, dimensions={0}, use_global_device_ids=true | all-gather | bytes 52224 | tf_op jit(solution)/shard_map/all_gather | solution.py:13
  167.1 29.4 %all-gather.7 = f32[16,12,64]{2,1,0:T(8,128)S(1)} all-gather(f32[1,12,64]{2,1,0:T(8,128)S(1)} %bitcast.119), channel_id=3, replica_groups=mesh['row'=16,'col'=16] {'col'}, dimensions={0}, use_global_device_ids=true | all-gather | bytes 52224 | tf_op jit(solution)/shard_map/all_gather | solution.py:13
  196.5 0.8 dynamic-slice_convert_fusion
  197.3 0.6 while.12
  197.8 31.0 %all-gather.12 = bf16[16,4,1536]{2,1,0:T(4,128)(2,1)S(1)} all-gather(bf16[1,4,1536]{2,1,0:T(4,128)(2,1)S(1)} %bitcast.120), channel_id=1, replica_groups=mesh['row'=16,'col'=16] {'col'}, dimensions={0}, use_global_device_ids=true | all-gather | bytes 208896 | tf_op jit(solution)/shard_map/all_gather | solution.py:97
  229.0 0.1 reshape.113
  229.2 1.7 fusion.28
  230.9 1.0 copy.90
  231.9 29.3 %all-gather.10 = bf16[16,4,288]{2,1,0:T(4,128)(2,1)S(1)} all-gather(bf16[1,4,288]{2,1,0:T(4,128)(2,1)S(1)} %bitcast.121), channel_id=1, replica_groups=mesh['row'=16,'col'=16] {'col'}, dimensions={0}, use_global_device_ids=true | all-gather | bytes 39168 | tf_op jit(solution)/shard_map/all_gather | solution.py:96
  261.5 46.3 %all-gather.11 = bf16[16,4,288]{2,1,0:T(4,128)(2,1)S(1)} all-gather(bf16[1,4,288]{2,1,0:T(4,128)(2,1)S(1)} %bitcast.122), channel_id=1, replica_groups=mesh['row'=16,'col'=16] {'row'}, dimensions={0}, use_global_device_ids=true | all-gather | bytes 39168 | tf_op jit(solution)/shard_map/all_gather | solution.py:90
  307.8 0.3 reshape.112
  308.1 30.7 %all-gather.8 = bf16[16,4,192]{2,1,0:T(4,128)(2,1)S(1)} all-gather(bf16[1,4,192]{2,1,0:T(4,128)(2,1)S(1)} %bitcast.127), channel_id=1, replica_groups=mesh['row'=16,'col'=16] {'col'}, dimensions={0}, use_global_device_ids=true | all-gather | bytes 26112 | tf_op jit(solution)/shard_map/all_gather | solution.py:95
  339.1 23.3 %all-gather.9 = bf16[16,4,192]{2,1,0:T(4,128)(2,1)S(1)} all-gather(bf16[1,4,192]{2,1,0:T(4,128)(2,1)S(1)} %bitcast.128), channel_id=1, replica_groups=mesh['row'=16,'col'=16] {'row'}, dimensions={0}, use_global_device_ids=true | all-gather | bytes 26112 | tf_op jit(solution)/shard_map/all_gather | solution.py:89
  362.3 0.9 reshape.110
  363.3 0.2 fusion.16
  363.4 2.1 multiply_reduce_fusion
  365.5 30.8 %psum.14 = f32[12,64]{1,0:T(8,128)} all-reduce(f32[12,64]{1,0:T(8,128)S(1)} %get-tuple-element.65), channel_id=1, replica_groups=mesh['row'=16,'col'=16] {'col'}, use_global_device_ids=true, to_apply=%region_7.8 | all-reduce | flops 768 | bytes 6144 | tf_op jit(solution)/shard_map/psum | solution.py:132
  396.3 1.9 convert_reduce_fusion
  398.2 1.0 convolution_multiply_fusion.2
  399.2 1.0 fusion.12
  400.4 0.7 pad_maximum_fusion.1
  401.1 0.2 all-reduce.7.cloned.1.call-start
  401.3 1.1 fusion.30
  402.4 1.7 fusion.29
  404.1 1.6 convolution_multiply_fusion.3
  405.9 1.6 copy.105
  407.5 0.2 fusion.13
  407.8 1.0 copy.103
  408.8 1.7 pad_maximum_fusion
  410.5 0.3 copy.107
  410.7 1.8 fusion.31
  412.6 0.3 copy.108
  412.9 5.9 multiply_add_fusion
  418.8 1.2 fusion.15
  420.0 0.6 dynamic-slice
  420.6 0.6 dynamic-slice.2
  422.4 81.4 %psum.15 = f32[128,12]{0,1:T(8,128)} all-reduce(f32[128,12]{0,1:T(8,128)S(1)} %fusion.15), channel_id=1, replica_groups=mesh['row'=16,'col'=16] {'row','col'}, use_global_device_ids=true, to_apply=%region_12.13 | all-reduce | flops 1536 | bytes 12288 | tf_op jit(solution)/shard_map/psum | solution.py:139
  503.8 35.9 %all-reduce.5.cloned.1.call-done = f32[64,336]{1,0:T(8,128)} async-done(((f32[64,336]{1,0:T(8,128)}), f32[64,336]{1,0:T(8,128)}) %all-reduce.5.cloned.1.call-update) | async-done | bytes 86032
  539.7 1.4 dynamic-slice.5
  541.0 1.3 constant_dynamic-slice_fusion.1
  542.3 124.8 %all-reduce.7.cloned.1.call-done = f32[64,816]{1,0:T(8,128)} async-done(((f32[64,816]{1,0:T(8,128)}), f32[64,816]{1,0:T(8,128)}) %all-reduce.7.cloned.1.call-update) | async-done | bytes 208912
  667.1 1.4 dynamic-slice.7
  668.5 1.4 fusion.25
  669.9 1.4 dynamic-slice.9
  (91 shorter events, 1.7 us)
Async XLA Ops:
  7.2 1.6 copy-start
  7.2 7.5 %copy-start.16 = (bf16[4,192]{1,0:T(4,128)(2,1)S(1)}, bf16[4,192]{1,0:T(4,128)(2,1)}, u32[]{:S(2)}) copy-start(bf16[4,192]{1,0:T(4,128)(2,1)} %param.17) | copy-start | bytes 4612
  7.2 532.5 %all-reduce.5.cloned.1.call-start = ((), (), s32[]{:S(2)}) async-start(), calls=%async_computation | async-start | bytes 196608
  7.2 45.7 %copy-start.17 = (bf16[4,192]{1,0:T(4,128)(2,1)S(1)}, bf16[4,192]{1,0:T(4,128)(2,1)}, u32[]{:S(2)}) copy-start(bf16[4,192]{1,0:T(4,128)(2,1)} %param.19) | copy-start | bytes 4612
  8.8 71.2 %copy-start.18 = (bf16[4,144]{1,0:T(4,128)(2,1)S(1)}, bf16[4,144]{1,0:T(4,128)(2,1)}, u32[]{:S(2)}) copy-start(bf16[4,144]{1,0:T(4,128)(2,1)} %param.18) | copy-start | bytes 3460
  8.8 100.6 %copy-start.19 = (bf16[4,144]{1,0:T(4,128)(2,1)S(1)}, bf16[4,144]{1,0:T(4,128)(2,1)}, u32[]{:S(2)}) copy-start(bf16[4,144]{1,0:T(4,128)(2,1)} %param.20) | copy-start | bytes 3460
  14.5 118.8 %copy-start.23 = (f32[12]{0:T(128)S(1)}, f32[12]{0:T(128)}, u32[]{:S(2)}) copy-start(f32[12]{0:T(128)} %param.25) | copy-start | bytes 148
  14.5 121.0 %copy-start.22 = (f32[12]{0:T(128)S(1)}, f32[12]{0:T(128)}, u32[]{:S(2)}) copy-start(f32[12]{0:T(128)} %param.26) | copy-start | bytes 148
  52.9 114.1 %copy-start.6 = (bf16[64,12,16]{0,2,1:T(8,128)(2,1)}, bf16[64,12,16]{0,2,1:T(8,128)(2,1)S(1)}, u32[]{:S(2)}) copy-start(bf16[64,12,16]{0,2,1:T(8,128)(2,1)S(1)} %copy.79) | copy-start | bytes 73732
  80.0 116.5 %copy-start.7 = (bf16[64,12,16]{0,2,1:T(8,128)(2,1)}, bf16[64,12,16]{0,2,1:T(8,128)(2,1)S(1)}, u32[]{:S(2)}) copy-start(bf16[64,12,16]{0,2,1:T(8,128)(2,1)S(1)} %copy.80) | copy-start | bytes 73732
  109.3 87.9 %copy-start.1 = (bf16[64,12,12]{0,2,1:T(8,128)(2,1)}, bf16[64,12,12]{0,2,1:T(8,128)(2,1)S(1)}, u32[]{:S(2)}) copy-start(bf16[64,12,12]{0,2,1:T(8,128)(2,1)S(1)} %copy.82) | copy-start | bytes 55300
  132.6 65.2 %copy-start.11 = (bf16[4,1536]{1,0:T(4,128)(2,1)S(1)}, bf16[4,1536]{1,0:T(4,128)(2,1)}, u32[]{:S(2)}) copy-start(bf16[4,1536]{1,0:T(4,128)(2,1)} %param.31) | copy-start | bytes 36868
  133.2 95.7 %copy-start.3 = (bf16[64,12,12]{0,2,1:T(8,128)(2,1)}, bf16[64,12,12]{0,2,1:T(8,128)(2,1)S(1)}, u32[]{:S(2)}) copy-start(bf16[64,12,12]{0,2,1:T(8,128)(2,1)S(1)} %copy.83) | copy-start | bytes 55300
  134.5 61.9 %copy-start.12 = (f32[64]{0:T(128)}, f32[64]{0:T(128)S(1)}, u32[]{:S(2)}) copy-start(f32[64]{0:T(128)S(1)} %get-tuple-element.55) | copy-start | bytes 772
  229.0 2.9 copy-start.13
  229.1 32.3 %copy-start.14 = (bf16[4,288]{1,0:T(4,128)(2,1)S(1)}, bf16[4,288]{1,0:T(4,128)(2,1)}, u32[]{:S(2)}) copy-start(bf16[4,288]{1,0:T(4,128)(2,1)} %param.22) | copy-start | bytes 6916
  229.1 79.0 %copy-start.20 = (bf16[4,192]{1,0:T(4,128)(2,1)S(1)}, bf16[4,192]{1,0:T(4,128)(2,1)}, u32[]{:S(2)}) copy-start(bf16[4,192]{1,0:T(4,128)(2,1)} %param.29) | copy-start | bytes 4612
  229.2 109.9 %copy-start.21 = (bf16[4,192]{1,0:T(4,128)(2,1)S(1)}, bf16[4,192]{1,0:T(4,128)(2,1)}, u32[]{:S(2)}) copy-start(bf16[4,192]{1,0:T(4,128)(2,1)} %param.21) | copy-start | bytes 4612
  261.4 134.9 %copy-start.5 = (bf16[64,288]{0,1:T(8,128)(2,1)}, bf16[64,288]{0,1:T(8,128)(2,1)S(1)}, u32[]{:S(2)}) copy-start(bf16[64,288]{0,1:T(8,128)(2,1)S(1)} %copy.88) | copy-start | bytes 110596
  339.0 57.3 %copy-start.8 = (bf16[64,192]{0,1:T(8,128)(2,1)}, bf16[64,192]{0,1:T(8,128)(2,1)S(1)}, u32[]{:S(2)}) copy-start(bf16[64,192]{0,1:T(8,128)(2,1)S(1)} %copy.86) | copy-start | bytes 73732
  398.2 9.3 %copy-start.2 = (bf16[64,12,12]{0,2,1:T(8,128)(2,1)S(1)}, bf16[64,12,12]{0,2,1:T(8,128)(2,1)}, u32[]{:S(2)}) copy-start(bf16[64,12,12]{0,2,1:T(8,128)(2,1)} %copy-done.1) | copy-start | bytes 55300
  398.2 9.3 %copy-start.4 = (bf16[64,12,12]{0,2,1:T(8,128)(2,1)S(1)}, bf16[64,12,12]{0,2,1:T(8,128)(2,1)}, u32[]{:S(2)}) copy-start(bf16[64,12,12]{0,2,1:T(8,128)(2,1)} %copy-done.3) | copy-start | bytes 55300
  398.2 9.3 %copy-start.10 = (f32[12,64]{1,0:T(8,128)S(1)}, f32[12,64]{1,0:T(8,128)}, u32[]{:S(2)}) copy-start(f32[12,64]{1,0:T(8,128)} %get-tuple-element.38) | copy-start | bytes 9220
  398.2 9.3 %copy-start.15 = (f32[12]{0:T(128)S(1)}, f32[12]{0:T(128)}, u32[]{:S(2)}) copy-start(f32[12]{0:T(128)} %get-tuple-element.61) | copy-start | bytes 148
  401.1 266.0 %all-reduce.7.cloned.1.call-start = ((), (), s32[]{:S(2)}) async-start(), calls=%async_computation.1 | async-start | bytes 458752
  410.5 2.4 copy-start.9
  418.7 1.2 copy-start.25
  418.8 1.8 copy-start.24
Sparse Core Ops, SparseCore 0:
  401.2 138.3 all-reduce.4
  542.5 124.5 all-reduce.6
where the time goes:
time: 679 us; the launch traced here: 678 us
  blocking collectives  449 us (66%)
  waiting for transfers between devices  161 us (24%)
  matrix products  25.8 us (4%)
  local copies, waits for them, and re-layouts  18.8 us (3%)
  between operations  15.8 us (2%)
  other arithmetic  7.09 us (1%)
    unnamed x4, waiting for transfers between devices  161 us
    psum x1, blocking collectives, on_device(): grad_bias_weight = lax.psum(weight_term, ('row', 'col'))  81.4 us
    all_gather x2, blocking collectives, merged(): pieces = jax.tree.map(lambda part: lax.all_gather(part, axis), value)  60.3 us
    all_gather x1, blocking collectives, on_device(): lax.all_gather(value_points, 'row', axis=0, tiled=True)  46.3 us
    all_gather x1, blocking collectives, on_device(): lax.all_gather(queries, 'col', axis=0, tiled=True)  37.8 us
    all_gather x1, blocking collectives, on_device(): lax.all_gather(cot_pair, 'col', axis=0, tiled=True)  31 us
    psum x1, blocking collectives, on_device(): dsum = lax.psum(jnp.sum(prob * dprob, -1), 'col')  30.8 us
    all_gather x1, blocking collectives, on_device(): lax.all_gather(cot_scalar, 'col', axis=0, tiled=True)  30.7 us
  transfers between devices with their start and end apart: 2, of which 2 were waited for; matrix products, arithmetic and copies ran while one was open for 3% of the time, Pallas kernels for 0%

commit v1 on v0

v1 whole, which is shorter than its diff:
```python
import math

import jax
import jax.numpy as jnp
from jax import lax
from jax.experimental import pallas as pl
from jax.experimental.pallas import tpu as pltpu
from jax.sharding import PartitionSpec as P

MESH = pl.DeviceIdType.MESH
NEG_FILL = -1e30
F32 = jnp.float32
BF16 = jnp.bfloat16
H = 12
HP = 16
TILE = 64
PEERS = 16
W_LOGIT = math.sqrt(1.0 / 3.0)
W_POINT = math.sqrt(2.0 / 36.0)
SCALE_Q = W_LOGIT / 4.0


def nt(a, b):
    return lax.dot_general(a, b, (((1,), (1,)), ((), ())), preferred_element_type=F32)


def nn(a, b):
    return lax.dot_general(a, b, (((1,), (0,)), ((), ())), preferred_element_type=F32)


def tn(a, b):
    return lax.dot_general(a, b, (((0,), (0,)), ((), ())), preferred_element_type=F32)


def exact_nn(a, b):
    return lax.dot_general(
        a, b, (((1,), (0,)), ((), ())), preferred_element_type=F32, precision=lax.Precision.HIGHEST
    )


def split(x):
    high = x.astype(BF16)
    return high, (x - high.astype(F32)).astype(BF16)


def head_masks(sub, lane):
    def block(col, width):
        return (col >= sub * width) & (col < sub * width + width)

    tiles = [
        block(lane, 16),
        ((lane < 64) & block(lane + 128, 16)) | (lane == sub + 64) | (lane == sub + 80),
        block(lane, 12),
        (lane < 16) & block(lane + 128, 12),
        block(lane, 16),
        block(lane, 24),
        block(lane + 128, 24),
        ((lane < 64) & block(lane + 128, 16)) | ((lane >= 64) & (lane < 96) & block(lane + 192, 24)),
    ]
    return [(tile & (sub < H)).astype(F32) for tile in tiles]


def kernel(
    q_in, qp_in, k_in, kp_in, v_in, vp_in, pair_in, bw_in, hw_in, cb_in, chain_in, live_in,
    gs_in, gp_in, gz_in,
    gq_out, gqp_out, gk_out, gkp_out, gv_out, gvp_out, gpair_out, gbw_out,
    q_v, qp_v, k_v, kp_v, v_v, vp_v, pair_v, bw_v, hw_s, cb_s, chain_s, live_s, chain_v, live_v,
    gs_v, gp_v, gz_v,
    pack, gz32, qsend, ksend, gzsend, qg, kg, gzg, blk,
    qf, kf, kdup, qbd, kbd, pp, base, qsq, expo, dprob, prob, dsr, dlo,
    stats, stat_send, stat_g, w_send, w_row, w_mid, w_col,
    kres, kch, kr, qres, qch, qr,
    in_sem, out_sem, send_sem, recv_sem,
):
    r = lax.axis_index("row")
    c = lax.axis_index("col")
    barrier = pltpu.get_barrier_semaphore()

    @pl.loop(1, PEERS)
    def _(s):
        pl.semaphore_signal(barrier, inc=1, device_id=(r, lax.rem(c + s, PEERS)), device_id_type=MESH)
        pl.semaphore_signal(barrier, inc=1, device_id=(lax.rem(r + s, PEERS), c), device_id_type=MESH)

    loads = [
        pltpu.make_async_copy(src, dst, in_sem.at[n])
        for n, (src, dst) in enumerate(
            (
                (pair_in, pair_v), (q_in, q_v), (qp_in, qp_v), (k_in, k_v), (kp_in, kp_v), (v_in, v_v),
                (vp_in, vp_v), (bw_in, bw_v), (hw_in, hw_s), (cb_in, cb_s), (chain_in, chain_s),
                (live_in, live_s), (chain_in, chain_v), (live_in, live_v), (gs_in, gs_v), (gp_in, gp_v),
                (gz_in, gz_v),
            )
        )
    ]
    for load in loads[1:]:
        load.start()
    loads[0].start()
    for load in loads[1:]:
        load.wait()

    sub = lax.broadcasted_iota(jnp.int32, (HP, 128), 0)
    lane = lax.broadcasted_iota(jnp.int32, (HP, 128), 1)
    left = lane < 64
    masks = head_masks(sub, lane)

    live4 = jnp.zeros((4, 128), F32)
    sub4 = lax.broadcasted_iota(jnp.int32, (4, 128), 0)
    first = r * TILE + c * 4
    for i in range(4):
        at = first + i
        live4 = jnp.where(sub4 == i, live_s[at // 128, lax.rem(at, 128)].astype(F32), live4)

    def pack_block(scalars, points, vals, vpoints, ones, live, send):
        pack[...] = jnp.zeros_like(pack)
        a, b = scalars[...].astype(F32), points[...].astype(F32)
        d, e = vals[...].astype(F32), vpoints[...].astype(F32)
        pack[0:4, :] = a[:, 0:128]
        pack[4:8, 0:64] = a[:, 128:192]
        pack[4:8, ones : ones + 16] = jnp.ones((4, 16), F32)
        pack[8:12, :] = b[:, 0:128]
        pack[12:16, 0:16] = b[:, 128:144]
        pack[16:20, :] = d[:, 0:128] * live
        pack[20:24, :] = e[:, 0:128] * live
        pack[24:28, :] = e[:, 128:256] * live
        pack[28:32, 0:64] = d[:, 128:192] * live[:, 0:64]
        pack[28:32, 64:96] = e[:, 256:288] * live[:, 0:32]
        send[...] = pack[...].astype(BF16)

    pack_block(q_v, qp_v, gs_v, gp_v, 64, live4, qsend)
    pack_block(k_v, kp_v, v_v, vp_v, 80, jnp.ones((4, 128), F32), ksend)
    gz32[...] = jnp.zeros_like(gz32)
    for h in range(H):
        gz32[pl.ds(h, 4, stride=HP), :] = gz_v[:, 128 * h : 128 * h + 128].astype(F32) * live4
    gzsend[...] = gz32[...].astype(BF16)
    qg[c] = qsend[...]
    kg[r] = ksend[...]
    gzg[c] = gzsend[...]

    ps = jnp.zeros((HP, 128), F32)
    cb = jnp.zeros((HP, 128), F32)
    for h in range(H):
        ps = jnp.where(sub == h, hw_s[h], ps)
        cb = jnp.where(sub == h, cb_s[h], cb)
    ps = W_LOGIT * ps * W_POINT / 2.0
    ps_lane = [jnp.sum(masks[t] * ps, 0, keepdims=True) for t in (2, 3)]
    bw_pad = jnp.concatenate((bw_v[...], jnp.zeros((128, 128 - H), F32)), 1)
    bw_t = jnp.transpose(bw_pad)[0:HP, :]
    bw_high, bw_low = split(bw_t)
    wb_high, wb_low = split(W_LOGIT * bw_t)
    col_at = c * TILE
    chain_k = chain_v[pl.ds(col_at // 128, 1), :]
    live_k = live_v[pl.ds(col_at // 128, 1), :].astype(F32)
    half = lax.rem(c, 2)
    lane1 = lax.broadcasted_iota(jnp.int32, (1, 128), 1)
    own = (lane1 // 64) == half
    chain_k = jnp.where(own, chain_k, pltpu.roll(chain_k, 64, 1))
    live_k = jnp.where(own, live_k, pltpu.roll(live_k, 64, 1))

    loads[0].wait()
    bias_lhs = jnp.concatenate(
        (jnp.concatenate((bw_high, bw_high), 1), jnp.concatenate((bw_low, bw_low), 1)), 0
    )

    @pl.loop(0, 16)
    def _(t):
        high, low = split(pair_v[pl.ds(256 * t, 256), :])
        both = jnp.concatenate((high, low), 1)
        pp[pl.ds(256 * t, 256), :] = both
        res = nt(bias_lhs, both)
        res = res[0:HP] + res[HP : 2 * HP]
        for a in range(2):
            at = r * TILE + 4 * t + 2 * a
            chain_q = jnp.where(
                lane1 < 64, chain_s[at // 128, lax.rem(at, 128)], chain_s[(at + 1) // 128, lax.rem(at + 1, 128)]
            )
            same = (chain_q == chain_k).astype(F32)
            base[pl.ds(32 * t + 16 * a, 16), :] = W_LOGIT * (res[:, 128 * a : 128 * a + 128] + cb * same)

    pl.semaphore_wait(barrier, 2 * (PEERS - 1))

    def spread(src, dst, axis, n):
        me = c if axis == "col" else r

        @pl.loop(1, PEERS)
        def _(s):
            to = lax.rem(me + s, PEERS)
            pltpu.make_async_remote_copy(
                src_ref=src,
                dst_ref=dst.at[me],
                send_sem=send_sem.at[n],
                recv_sem=recv_sem.at[n],
                device_id=(r, to) if axis == "col" else (to, c),
                device_id_type=MESH,
            ).start()

    def scatter(src, dst, axis, n):
        me = c if axis == "col" else r

        @pl.loop(1, PEERS)
        def _(s):
            to = lax.rem(me + s, PEERS)
            pltpu.make_async_remote_copy(
                src_ref=src.at[to],
                dst_ref=dst.at[me],
                send_sem=send_sem.at[n],
                recv_sem=recv_sem.at[n],
                device_id=(r, to) if axis == "col" else (to, c),
                device_id_type=MESH,
            ).start()

    def wait_recv(dst, n):
        part = dst.at[pl.ds(0, PEERS - 1)]
        pltpu.make_async_copy(part, part, recv_sem.at[n]).wait()

    def wait_send(dst, n):
        part = dst.at[pl.ds(0, PEERS - 1)]
        pltpu.make_async_copy(part, part, send_sem.at[n]).wait()

    spread(qsend, qg, "col", 0)
    spread(ksend, kg, "row", 1)
    spread(gzsend, gzg, "col", 2)

    def assemble(got, full):
        blk[...] = got[...].astype(F32)
        for s in range(PEERS):
            for t in range(8):
                full[4 * s : 4 * s + 4, 128 * t : 128 * t + 128] = blk[s, 4 * t : 4 * t + 4, :]

    wait_recv(kg, 1)
    assemble(kg, kf)
    kb = kf[...].astype(BF16)
    kdup[0:TILE, :] = kb
    kdup[TILE : 2 * TILE, :] = kb
    for h in range(H):
        for t in range(4):
            kbd[TILE * h : TILE * h + TILE, 128 * t : 128 * t + 128] = (
                kf[:, 128 * t : 128 * t + 128] * masks[t][h : h + 1, :]
            ).astype(BF16)
    kp_sq_high, kp_sq_low = split(kf[:, 256:512] * kf[:, 256:512])
    point_mask = jnp.concatenate((masks[2], masks[3]), 1)
    point_mask16 = point_mask.astype(BF16)
    k_sq = nt(point_mask16, kp_sq_high) + nt(point_mask16, kp_sq_low)
    k_sq = jnp.concatenate((k_sq, k_sq), 1)

    wait_recv(qg, 0)
    assemble(qg, qf)

    @pl.loop(0, 8)
    def _(b):
        eight = qf[pl.ds(pl.multiple_of(8 * b, 8), 8), :]
        for p in range(4):
            rows = pl.ds(64 * b + HP * p, HP)
            sums = []
            for odd in range(2):
                square = jnp.zeros((HP, 128), F32)
                for t in range(8):
                    value = eight[2 * p + odd : 2 * p + odd + 1, 128 * t : 128 * t + 128] * masks[t]
                    qbd[odd, rows, 128 * t : 128 * t + 128] = value.astype(BF16)
                    if t in (2, 3):
                        square = square + value * value
                sums.append(jnp.sum(square, 1, keepdims=True))
            qsq[rows, :] = jnp.where(left, sums[0], sums[1])

    stats[...] = jnp.zeros_like(stats)
    lane3 = lax.broadcasted_iota(jnp.int32, (8, HP, 128), 2)
    left3 = lane3 < 64

    @pl.loop(0, 4)
    def _(b):
        rows = pl.ds(128 * b, 128)
        parts = []
        for k0, k1 in ((0, 256), (256, 512), (512, 1024)):
            even = nt(qbd[0, rows, k0:k1], kdup[:, k0:k1]).reshape(8, HP, 128)
            odd = nt(qbd[1, rows, k0:k1], kdup[:, k0:k1]).reshape(8, HP, 128)
            parts.append(jnp.where(left3, even, odd))
        dprob[rows, :] = parts[2].reshape(128, 128)
        distance = qsq[rows, :].reshape(8, HP, 128) + k_sq - 2.0 * parts[1]
        logits = base[rows, :].reshape(8, HP, 128) + SCALE_Q * parts[0] - ps * distance
        logits = jnp.where(live_k > 0, logits, NEG_FILL)
        max0 = jnp.max(jnp.where(left3, logits, NEG_FILL), 2, keepdims=True)
        max1 = jnp.max(jnp.where(left3, NEG_FILL, logits), 2, keepdims=True)
        e = jnp.exp(logits - jnp.where(left3, max0, max1)) * live_k
        sum0 = jnp.sum(jnp.where(left3, e, 0.0), 2, keepdims=True)
        sum1 = jnp.sum(jnp.where(left3, 0.0, e), 2, keepdims=True)
        expo[rows, :] = e.reshape(128, 128)
        acc_m, acc_s = stats[0], stats[1]
        for i in range(8):
            at = 16 * b + 2 * i
            acc_m = jnp.where(lane == at, max0[i], jnp.where(lane == at + 1, max1[i], acc_m))
            acc_s = jnp.where(lane == at, sum0[i], jnp.where(lane == at + 1, sum1[i], acc_s))
        stats[0] = acc_m
        stats[1] = acc_s

    wait_recv(gzg, 2)

    @pl.loop(0, 16)
    def _(t):
        gz = gzg[t]
        res = nt(jnp.concatenate((gz, gz), 1), pp[pl.ds(256 * t, 256), :])
        acc = stats[2]
        for a in range(2):
            rows = pl.ds(32 * t + 16 * a, 16)
            tile = res[32 * a : 32 * a + 32, 128 * a : 128 * a + 128]
            value = dprob[rows, :] + jnp.where(left, tile[0:16], tile[16:32])
            dprob[rows, :] = value
            weighted = expo[rows, :] * value
            sum0 = jnp.sum(jnp.where(left, weighted, 0.0), 1, keepdims=True)
            sum1 = jnp.sum(jnp.where(left, 0.0, weighted), 1, keepdims=True)
            at = 4 * t + 2 * a
            acc = jnp.where(lane == at, sum0, jnp.where(lane == at + 1, sum1, acc))
        stats[2] = acc

    row_max, row_sum = stats[0], stats[1]
    any_live = row_sum > 0
    safe = jnp.where(any_live, row_sum, 1.0)
    lse = jnp.where(any_live, row_max + jnp.log(safe), NEG_FILL)
    mean = jnp.where(any_live, stats[2] / safe, 0.0)
    stat_send[...] = jnp.where(left, lse, pltpu.roll(mean, 64, 1))
    stat_g[c] = stat_send[...]
    spread(stat_send, stat_g, "col", 3)
    wait_recv(stat_g, 3)
    top = stat_g[0]
    for s in range(1, PEERS):
        top = jnp.maximum(top, stat_g[s])
    total = jnp.zeros((HP, 128), F32)
    dsum = jnp.zeros((HP, 128), F32)
    for s in range(PEERS):
        got = stat_g[s]
        weight = jnp.exp(got - top)
        total = total + weight
        dsum = dsum + weight * pltpu.roll(got, 64, 1)
    stats[0] = jnp.exp(row_max - top) / total
    stats[1] = dsum / total

    @pl.loop(0, 8)
    def _(b):
        scale = pltpu.roll(stats[0], lax.rem(128 - 8 * b, 128), 1)
        mean_all = pltpu.roll(stats[1], lax.rem(128 - 8 * b, 128), 1)
        for i in range(4):
            rows = pl.ds(64 * b + 16 * i, 16)
            factor = jnp.where(left, scale[:, 2 * i : 2 * i + 1], scale[:, 2 * i + 1 : 2 * i + 2])
            shift = jnp.where(left, mean_all[:, 2 * i : 2 * i + 1], mean_all[:, 2 * i + 1 : 2 * i + 2])
            p = expo[rows, :] * factor
            ds = p * (dprob[rows, :] - shift)
            high, low = split(ds)
            prob[rows, :] = p.astype(BF16).astype(F32)
            dsr[rows, :] = high.astype(F32)
            dlo[rows, :] = low

    def weight_step(t, acc):
        high = dsr[pl.ds(32 * t, 32), :].astype(BF16)
        low = dlo[pl.ds(32 * t, 32), :]
        lhs = jnp.concatenate(
            (
                jnp.concatenate((high[0:16], high[16:32]), 1),
                jnp.concatenate((low[0:16], low[16:32]), 1),
            ),
            0,
        )
        return acc + nn(lhs, pp[pl.ds(256 * t, 256), :])

    w_all = lax.fori_loop(0, 16, weight_step, jnp.zeros((2 * HP, 256), F32))
    w_all = w_all[:, 0:128] + w_all[:, 128:256]
    w_send[...] = W_LOGIT * (w_all[0:HP] + w_all[HP : 2 * HP])
    w_row[r] = w_send[...]
    spread(w_send, w_row, "row", 4)

    ds_t = jnp.transpose(dsr[...]).astype(BF16)
    prob_t = jnp.transpose(prob[...]).astype(BF16)
    kside = nn(ds_t[0:TILE], qbd[0, :, 0:512]) + nn(ds_t[TILE : 2 * TILE], qbd[1, :, 0:512])
    vside = nn(prob_t[0:TILE], qbd[0, :, 512:1024]) + nn(prob_t[TILE : 2 * TILE], qbd[1, :, 512:1024])
    expand_q = jnp.concatenate((jnp.zeros((64, 256), F32), point_mask, jnp.zeros((48, 256), F32)), 0)
    expand_k = jnp.concatenate((jnp.zeros((80, 256), F32), point_mask, jnp.zeros((32, 256), F32)), 0)
    ps_row = jnp.concatenate(ps_lane, 1)
    kres[:, 0:256] = SCALE_Q * kside[:, 0:256]
    kres[:, 256:512] = -2.0 * ps_row * (
        exact_nn(kside[:, 128:256], expand_q) * kf[:, 256:512] - kside[:, 256:512]
    )
    kres[:, 512:1024] = vside
    for s in range(PEERS):
        for t in range(8):
            kch[s, 4 * t : 4 * t + 4, :] = kres[4 * s : 4 * s + 4, 128 * t : 128 * t + 128]
    kr[r] = kch[r]
    scatter(kch, kr, "row", 5)

    left32 = lax.broadcasted_iota(jnp.int32, (32, 128), 1) < 64
    evens, odds = [], []
    for pairing in range(H // 2):
        one = dsr[pl.ds(2 * pairing, 32, stride=HP), :]
        two = dsr[pl.ds(2 * pairing + 1, 32, stride=HP), :]
        evens.append(jnp.where(left32, one, pltpu.roll(two, 64, 1)).astype(BF16))
        odds.append(jnp.where(left32, pltpu.roll(one, 64, 1), two).astype(BF16))
    lhs = jnp.concatenate((jnp.concatenate(evens, 1), jnp.concatenate(odds, 1)), 0)
    qside = nn(lhs, kbd[...])
    for t in range(4):
        for odd in range(2):
            qres[t, pl.ds(odd, 32, stride=2), :] = qside[32 * odd : 32 * odd + 32, 128 * t : 128 * t + 128]
    row_sums = exact_nn(qres[1], expand_k)
    for t in (2, 3):
        at = 128 * (t - 2)
        qres[t] = -2.0 * ps_lane[t - 2] * (
            row_sums[:, at : at + 128] * qf[:, 128 * t : 128 * t + 128] - qres[t]
        )
    for t in (0, 1):
        qres[t] = SCALE_Q * qres[t]
    for s in range(PEERS):
        for t in range(4):
            qch[s, 4 * t : 4 * t + 4, :] = qres[t, 4 * s : 4 * s + 4, :]
    qr[c] = qch[c]
    scatter(qch, qr, "col", 6)

    wait_recv(w_row, 4)
    w_sum = w_row[0]
    for s in range(1, PEERS):
        w_sum = w_sum + w_row[s]
    w_mid[...] = w_sum
    w_col[c] = w_sum
    spread(w_mid, w_col, "col", 7)

    wb = jnp.concatenate((wb_high, wb_high, wb_low), 0)
    writes = [
        pltpu.make_async_copy(
            pair_v.at[pl.ds(1024 * n, 1024)], gpair_out.at[pl.ds(1024 * n, 1024)], out_sem.at[n]
        )
        for n in range(4)
    ]
    for n in range(4):

        @pl.loop(4 * n, 4 * n + 4)
        def _(t):
            gz = gzg[t]
            for a in range(2):
                rows = pl.ds(32 * t + 16 * a, 16)
                p = prob[rows, :]
                high = dsr[rows, :].astype(BF16)
                lhs = jnp.concatenate(
                    (
                        jnp.where(left, p, 0.0).astype(BF16),
                        jnp.where(left, 0.0, p).astype(BF16),
                        high,
                        dlo[rows, :],
                        high,
                    ),
                    0,
                )
                rhs = jnp.concatenate((gz[32 * a : 32 * a + 32], wb), 0)
                pair_v[pl.ds(256 * t + 128 * a, 128), :] = tn(lhs, rhs)

        writes[n].start()

    wait_recv(kr, 5)
    ksum = kr[0]
    for s in range(1, PEERS):
        ksum = ksum + kr[s]
    gk_out[:, 0:128] = ksum[0:4]
    gk_out[:, 128:192] = ksum[4:8, 0:64]
    gkp_out[:, 0:128] = ksum[8:12]
    gkp_out[:, 128:144] = ksum[12:16, 0:16]
    gv_out[:, 0:128] = ksum[16:20]
    gv_out[:, 128:192] = ksum[28:32, 0:64]
    gvp_out[:, 0:128] = ksum[20:24]
    gvp_out[:, 128:256] = ksum[24:28]
    gvp_out[:, 256:288] = ksum[28:32, 64:96]
    wait_recv(qr, 6)
    qsum = qr[0]
    for s in range(1, PEERS):
        qsum = qsum + qr[s]
    gq_out[:, 0:128] = qsum[0:4]
    gq_out[:, 128:192] = qsum[4:8, 0:64]
    gqp_out[:, 0:128] = qsum[8:12]
    gqp_out[:, 128:144] = qsum[12:16, 0:16]

    wait_recv(w_col, 7)
    w_sum = w_col[0]
    for s in range(1, PEERS):
        w_sum = w_sum + w_col[s]
    w_full = jnp.concatenate((w_sum, jnp.zeros((128 - HP, 128), F32)), 0)
    gbw_out[...] = jnp.transpose(w_full)[:, 0:H]

    for n, dst in enumerate((qg, kg, gzg, stat_g, w_row, kr, qr, w_col)):
        wait_send(dst, n)
    for write in writes:
        write.wait()


def on_device(
    queries, query_points, key_feats, key_points, values, value_points, pair_rep, bias_weight,
    head_weight, chain_bias, chain_ids, live_mask, cot_scalar, cot_points, cot_pair,
):
    any_spec = pl.BlockSpec(memory_space=pl.ANY)
    vmem_spec = pl.BlockSpec(memory_space=pltpu.VMEM)

    def vm(*shape, kind=F32):
        return pltpu.VMEM(shape, kind)

    scratch = [
        vm(4, 192, kind=BF16), vm(4, 144, kind=BF16), vm(4, 192, kind=BF16), vm(4, 144, kind=BF16),
        vm(4, 192, kind=BF16), vm(4, 288, kind=BF16), vm(4096, 128), vm(128, H),
        pltpu.SMEM((H,), F32), pltpu.SMEM((H,), F32),
        pltpu.SMEM((8, 128), jnp.int32), pltpu.SMEM((8, 128), jnp.int32),
        vm(8, 128, kind=jnp.int32), vm(8, 128, kind=jnp.int32),
        vm(4, 192, kind=BF16), vm(4, 288, kind=BF16), vm(4, 1536, kind=BF16),
        vm(32, 128), vm(64, 128), vm(32, 128, kind=BF16), vm(32, 128, kind=BF16), vm(64, 128, kind=BF16),
        vm(PEERS, 32, 128, kind=BF16), vm(PEERS, 32, 128, kind=BF16), vm(PEERS, 64, 128, kind=BF16),
        vm(PEERS, 32, 128),
        vm(TILE, 1024), vm(TILE, 1024), vm(2 * TILE, 1024, kind=BF16), vm(2, 512, 1024, kind=BF16),
        vm(H * TILE, 512, kind=BF16), vm(4096, 256, kind=BF16), vm(512, 128), vm(512, 128), vm(512, 128),
        vm(512, 128), vm(512, 128), vm(512, 128), vm(512, 128, kind=BF16),
        vm(3, HP, 128), vm(HP, 128), vm(PEERS, HP, 128), vm(HP, 128), vm(PEERS, HP, 128), vm(HP, 128),
        vm(PEERS, HP, 128),
        vm(TILE, 1024), vm(PEERS, 32, 128), vm(PEERS, 32, 128), vm(4, TILE, 128), vm(PEERS, 16, 128),
        vm(PEERS, 16, 128),
        pltpu.SemaphoreType.DMA((17,)), pltpu.SemaphoreType.DMA((4,)),
        pltpu.SemaphoreType.DMA((8,)), pltpu.SemaphoreType.DMA((8,)),
    ]
    out_shape = [
        jax.ShapeDtypeStruct(shape, F32)
        for shape in ((4, 192), (4, 144), (4, 192), (4, 144), (4, 192), (4, 288), (4096, 128), (128, H))
    ]
    out = pl.pallas_call(
        kernel,
        out_shape=out_shape,
        in_specs=[any_spec] * 15,
        out_specs=[vmem_spec] * 6 + [any_spec, vmem_spec],
        scratch_shapes=scratch,
        compiler_params=pltpu.CompilerParams(
            collective_id=0, has_side_effects=True, vmem_limit_bytes=40 * 2**20
        ),
        cost_estimate=pl.CostEstimate(flops=10**9, bytes_accessed=5 * 2**20, transcendentals=10**5),
    )(
        queries, query_points, key_feats, key_points, values, value_points,
        pair_rep.reshape(4096, 128), bias_weight, head_weight, chain_bias,
        chain_ids.reshape(8, 128), live_mask.reshape(8, 128), cot_scalar, cot_points, cot_pair,
    )
    return (*out[:6], out[6].reshape(TILE, TILE, 128), out[7])


def solution(mesh):
    rc, cr = P(("row", "col"), None), P(("col", "row"), None)
    tile = P("row", "col", None)
    return jax.shard_map(
        on_device,
        mesh=mesh,
        in_specs=(rc, rc, cr, cr, cr, cr, tile, P(), P(), P(), P(), P(), rc, rc, rc),
        out_specs=(rc, rc, cr, cr, cr, cr, tile, P()),
        check_vma=False,
    )
```

time: 679 us -> 67.4 us (0.10)
  blocking collectives: 449 us -> 0 us
  waiting for transfers between devices: 161 us -> 0 us
  Pallas kernels: 0 us -> 49.5 us
  matrix products: 25.8 us -> 0 us
  between operations: 15.8 us -> 0.66 us
  other arithmetic: 7.09 us -> 0 us
    all_gather x11 -> x0, blocking collectives: 337 us -> none  [the longest x2 60.3 us: merged(): pieces = jax.tree.map(lambda part: lax.all_gather(part, axis), value)]
    unnamed x4 -> x0, waiting for transfers between devices: 161 us -> none
    psum x2 -> x0, blocking collectives: 112 us -> none  [the longest x1 81.4 us: on_device(): grad_bias_weight = lax.psum(weight_term, ('row', 'col'))]
    pallas_call x0 -> x1, Pallas kernels: none -> 49.5 us  [on_device(): pl.pallas_call(kernel, out_shape=out_shape, in_specs=[any_spec] * 15, out...]
    dot_general x15 -> x0, matrix products: 25.8 us -> none  [the longest x1 5.89 us: on_device(): jnp.einsum('hij,ch->ijc', dscore, bias_weight, precision=HIGH)]
    unnamed x57 -> x37, local copies, waits for them, and re-layouts: 2.9 us -> 16.8 us
    slice x9 -> x0, local copies, waits for them, and re-layouts: 6.81 us -> none  [the longest x1 1.38 us: on_device(): grad_values = key_side[:, width_s + width_q:2 * width_s + width_q]]
  transfers between devices with their start and end apart: 2 -> 0, of which waited for: 2 -> 0; matrix products, arithmetic and copies ran while one was open for 3% -> 0% of each run, Pallas kernels for 0% -> 0%
where the time goes in v1:
time: 67.4 us; the launch traced here: 66.9 us
  Pallas kernels  49.5 us (73%)
  local copies, waits for them, and re-layouts  16.8 us (25%)
    pallas_call x1, Pallas kernels, on_device(): pl.pallas_call(kernel, out_shape=out_shape, in_specs=[any_spec] * 15, out...  49.5 us
    unnamed x37, local copies, waits for them, and re-layouts  16.8 us

profile of v1, /device:TPU:1, one launch (start us, length us, event | category | flops | bytes accessed | tf_op | source)
XLA Modules:
  0.0 66.9 jit_solution(1750287457367983551)
XLA Ops:
  0.6 0.8 %copy.23.bw_in = f32[128,12]{1,0:T(8,128)S(1)} copy(f32[128,12]{0,1:T(8,128)} %param.22) | data formatting | bytes 12288 | tf_op args[7]
  1.4 0.0 copy-start
  1.4 1.6 %copy-done = f32[64,64,128]{2,1,0:T(8,128)S(1)} copy-done((f32[64,64,128]{2,1,0:T(8,128)S(1)}, f32[64,64,128]{2,1,0:T(8,128)}, u32[]{:S(2)}) %copy-start) | copy-done | bytes 2097176
  3.0 0.0 copy-start.1
  3.0 0.7 %copy-done.1 = bf16[4,1536]{1,0:T(4,128)(2,1)S(1)} copy-done((bf16[4,1536]{1,0:T(4,128)(2,1)S(1)}, bf16[4,1536]{1,0:T(4,128)(2,1)}, u32[]{:S(2)}) %copy-start.1) | copy-done | bytes 12312
  3.7 0.0 copy-start.2
  3.7 0.7 %copy-done.2 = s32[1024]{0:T(1024)S(1)} copy-done((s32[1024]{0:T(1024)S(1)}, s32[1024]{0:T(1024)}, u32[]{:S(2)}) %copy-start.2) | copy-done | bytes 4120
  4.4 0.0 copy-start.3
  4.4 0.7 %copy-done.3 = s32[1024]{0:T(1024)S(1)} copy-done((s32[1024]{0:T(1024)S(1)}, s32[1024]{0:T(1024)}, u32[]{:S(2)}) %copy-start.3) | copy-done | bytes 4120
  5.1 0.0 copy-start.4
  5.1 0.7 %copy-done.4 = bf16[4,288]{1,0:T(4,128)(2,1)S(1)} copy-done((bf16[4,288]{1,0:T(4,128)(2,1)S(1)}, bf16[4,288]{1,0:T(4,128)(2,1)}, u32[]{:S(2)}) %copy-start.4) | copy-done | bytes 2328
  5.8 0.0 copy-start.5
  5.8 0.7 %copy-done.5 = bf16[4,288]{1,0:T(4,128)(2,1)S(1)} copy-done((bf16[4,288]{1,0:T(4,128)(2,1)S(1)}, bf16[4,288]{1,0:T(4,128)(2,1)}, u32[]{:S(2)}) %copy-start.5) | copy-done | bytes 2328
  6.5 0.0 copy-start.6
  6.5 0.7 %copy-done.6 = bf16[4,192]{1,0:T(4,128)(2,1)S(1)} copy-done((bf16[4,192]{1,0:T(4,128)(2,1)S(1)}, bf16[4,192]{1,0:T(4,128)(2,1)}, u32[]{:S(2)}) %copy-start.6) | copy-done | bytes 1560
  7.2 0.0 copy-start.7
  7.2 0.7 %copy-done.7 = bf16[4,144]{1,0:T(4,128)(2,1)S(1)} copy-done((bf16[4,144]{1,0:T(4,128)(2,1)S(1)}, bf16[4,144]{1,0:T(4,128)(2,1)}, u32[]{:S(2)}) %copy-start.7) | copy-done | bytes 1176
  7.8 0.0 copy-start.8
  7.8 0.7 %copy-done.8 = bf16[4,192]{1,0:T(4,128)(2,1)S(1)} copy-done((bf16[4,192]{1,0:T(4,128)(2,1)S(1)}, bf16[4,192]{1,0:T(4,128)(2,1)}, u32[]{:S(2)}) %copy-start.8) | copy-done | bytes 1560
  8.5 0.0 copy-start.9
  8.5 0.7 %copy-done.9 = bf16[4,144]{1,0:T(4,128)(2,1)S(1)} copy-done((bf16[4,144]{1,0:T(4,128)(2,1)S(1)}, bf16[4,144]{1,0:T(4,128)(2,1)}, u32[]{:S(2)}) %copy-start.9) | copy-done | bytes 1176
  9.2 0.0 copy-start.10
  9.2 0.7 %copy-done.10 = bf16[4,192]{1,0:T(4,128)(2,1)S(1)} copy-done((bf16[4,192]{1,0:T(4,128)(2,1)S(1)}, bf16[4,192]{1,0:T(4,128)(2,1)}, u32[]{:S(2)}) %copy-start.10) | copy-done | bytes 1560
  9.9 0.0 copy-start.11
  9.9 0.7 %copy-done.11 = bf16[4,192]{1,0:T(4,128)(2,1)S(1)} copy-done((bf16[4,192]{1,0:T(4,128)(2,1)S(1)}, bf16[4,192]{1,0:T(4,128)(2,1)}, u32[]{:S(2)}) %copy-start.11) | copy-done | bytes 1560
  10.6 0.0 copy-start.12
  10.6 0.7 copy-done.12
  11.2 0.0 copy-start.13
  11.2 0.7 copy-done.13
  11.9 49.5 %shard_map.206 = (f32[4,192]{1,0:T(4,128)S(1)}, f32[4,144]{1,0:T(4,128)S(1)}, f32[4,192]{1,0:T(4,128)S(1)}, f32[4,144]{1,0:T(4,128)S(1)}, f32[4,192]{1,0:T(4,128...) custom-call(bf16[4,192]{1,0:T(4,128)(2,1)S(1)} %copy-done.6, ...), custom_call_target="tpu_custom_call" | custom-call | flops 1000000000 | bytes 5242880 | tf_op jit(solution)/shard_map/pallas_call | solution.py:520
  61.4 0.7 %copy.24 = f32[128,12]{0,1:T(8,128)} copy(f32[128,12]{1,0:T(8,128)S(1)} %get-tuple-element.31) | data formatting | bytes 12288
  62.1 0.6 copy.32
  62.6 0.6 copy.33
  63.2 0.6 copy.34
  63.8 0.6 copy.35
  64.4 0.6 copy.36
  65.0 0.6 copy.37
  65.6 1.3 %copy.38 = f32[64,64,128]{2,1,0:T(8,128)} copy(f32[64,64,128]{2,1,0:T(8,128)S(1)} %bitcast.4) | data formatting | bytes 4194304
Async XLA Ops:
  1.4 1.6 %copy-start = (f32[64,64,128]{2,1,0:T(8,128)S(1)}, f32[64,64,128]{2,1,0:T(8,128)}, u32[]{:S(2)}) copy-start(f32[64,64,128]{2,1,0:T(8,128)} %param.21) | copy-start | bytes 6291460
  3.0 0.7 %copy-start.1 = (bf16[4,1536]{1,0:T(4,128)(2,1)S(1)}, bf16[4,1536]{1,0:T(4,128)(2,1)}, u32[]{:S(2)}) copy-start(bf16[4,1536]{1,0:T(4,128)(2,1)} %gz_in.1) | copy-start | bytes 36868
  3.7 0.7 %copy-start.2 = (s32[1024]{0:T(1024)S(1)}, s32[1024]{0:T(1024)}, u32[]{:S(2)}) copy-start(s32[1024]{0:T(1024)} %param.25) | copy-start | bytes 12292
  4.4 0.7 %copy-start.3 = (s32[1024]{0:T(1024)S(1)}, s32[1024]{0:T(1024)}, u32[]{:S(2)}) copy-start(s32[1024]{0:T(1024)} %param.26) | copy-start | bytes 12292
  5.1 0.7 %copy-start.4 = (bf16[4,288]{1,0:T(4,128)(2,1)S(1)}, bf16[4,288]{1,0:T(4,128)(2,1)}, u32[]{:S(2)}) copy-start(bf16[4,288]{1,0:T(4,128)(2,1)} %vp_in.1) | copy-start | bytes 6916
  5.8 0.7 %copy-start.5 = (bf16[4,288]{1,0:T(4,128)(2,1)S(1)}, bf16[4,288]{1,0:T(4,128)(2,1)}, u32[]{:S(2)}) copy-start(bf16[4,288]{1,0:T(4,128)(2,1)} %gp_in.1) | copy-start | bytes 6916
  6.5 0.7 %copy-start.6 = (bf16[4,192]{1,0:T(4,128)(2,1)S(1)}, bf16[4,192]{1,0:T(4,128)(2,1)}, u32[]{:S(2)}) copy-start(bf16[4,192]{1,0:T(4,128)(2,1)} %q_in.1) | copy-start | bytes 4612
  7.2 0.7 %copy-start.7 = (bf16[4,144]{1,0:T(4,128)(2,1)S(1)}, bf16[4,144]{1,0:T(4,128)(2,1)}, u32[]{:S(2)}) copy-start(bf16[4,144]{1,0:T(4,128)(2,1)} %qp_in.1) | copy-start | bytes 3460
  7.8 0.7 %copy-start.8 = (bf16[4,192]{1,0:T(4,128)(2,1)S(1)}, bf16[4,192]{1,0:T(4,128)(2,1)}, u32[]{:S(2)}) copy-start(bf16[4,192]{1,0:T(4,128)(2,1)} %k_in.1) | copy-start | bytes 4612
  8.5 0.7 %copy-start.9 = (bf16[4,144]{1,0:T(4,128)(2,1)S(1)}, bf16[4,144]{1,0:T(4,128)(2,1)}, u32[]{:S(2)}) copy-start(bf16[4,144]{1,0:T(4,128)(2,1)} %kp_in.1) | copy-start | bytes 3460
  9.2 0.7 %copy-start.10 = (bf16[4,192]{1,0:T(4,128)(2,1)S(1)}, bf16[4,192]{1,0:T(4,128)(2,1)}, u32[]{:S(2)}) copy-start(bf16[4,192]{1,0:T(4,128)(2,1)} %v_in.1) | copy-start | bytes 4612
  9.9 0.7 %copy-start.11 = (bf16[4,192]{1,0:T(4,128)(2,1)S(1)}, bf16[4,192]{1,0:T(4,128)(2,1)}, u32[]{:S(2)}) copy-start(bf16[4,192]{1,0:T(4,128)(2,1)} %gs_in.1) | copy-start | bytes 4612
  10.6 0.7 copy-start.12
  11.2 0.7 copy-start.13

commit v2 on v1

--- a/solution.py
+++ b/solution.py
@@ -15,13 +15,11 @@
 HP = 16
 TILE = 64
 PEERS = 16
+VMEM_LIMIT = 60 * 2**20
+CHUNKS = 8
 W_LOGIT = math.sqrt(1.0 / 3.0)
 W_POINT = math.sqrt(2.0 / 36.0)
 SCALE_Q = W_LOGIT / 4.0
-
-
-def nt(a, b):
-    return lax.dot_general(a, b, (((1,), (1,)), ((), ())), preferred_element_type=F32)
 
 
 def nn(a, b):
@@ -66,20 +64,60 @@
     gq_out, gqp_out, gk_out, gkp_out, gv_out, gvp_out, gpair_out, gbw_out,
     q_v, qp_v, k_v, kp_v, v_v, vp_v, pair_v, bw_v, hw_s, cb_s, chain_s, live_s, chain_v, live_v,
     gs_v, gp_v, gz_v,
-    pack, gz32, qsend, ksend, gzsend, qg, kg, gzg, blk,
-    qf, kf, kdup, qbd, kbd, pp, base, qsq, expo, dprob, prob, dsr, dlo,
+    pack, gz32, qsend, ksend, gzsend, qg, kg, gzg, blk, gz12, gz16, gzp,
+    qf, kf, kdup, qbd, kbd, pp, ppt, base, qsq, expo, dprob, prob, dsr, dlo,
     stats, stat_send, stat_g, w_send, w_row, w_mid, w_col,
     kres, kch, kr, qres, qch, qr,
+    gq_v, gqp_v, gk_v, gkp_v, gv_v, gvp_v, gbw_v,
     in_sem, out_sem, send_sem, recv_sem,
 ):
     r = lax.axis_index("row")
     c = lax.axis_index("col")
     barrier = pltpu.get_barrier_semaphore()
 
-    @pl.loop(1, PEERS)
-    def _(s):
-        pl.semaphore_signal(barrier, inc=1, device_id=(r, lax.rem(c + s, PEERS)), device_id_type=MESH)
-        pl.semaphore_signal(barrier, inc=1, device_id=(lax.rem(r + s, PEERS), c), device_id_type=MESH)
+    def fan(axis, act):
+        if axis == "col":
+            y, z = c // 8, lax.rem(c, 8)
+
+            def at(dy, j):
+                dz = 4 + (1 - 2 * lax.rem(j, 2)) * ((j + 1) // 2)
+                act((r, lax.rem(y + dy, 2) * 8 + lax.rem(z + dz, 8)))
+
+            @pl.loop(0, 3)
+            def _(j):
+                at(1, j)
+
+            @pl.loop(3, 8)
+            def _(j):
+                at(1, j)
+                at(0, j - 3)
+
+            @pl.loop(5, 7)
+            def _(j):
+                at(0, j)
+        else:
+            x, y, core = r // 4, lax.rem(r // 2, 2), lax.rem(r, 2)
+
+            def at(dx, dy, dc):
+                act((lax.rem(x + dx, 4) * 4 + lax.rem(y + dy, 2) * 2 + lax.rem(core + dc, 2), c))
+
+            @pl.loop(0, 3)
+            def _(m):
+                dx = 2 + (1 - 2 * lax.rem(m, 2)) * ((m + 1) // 2)
+                at(dx, 1, 1)
+                at(dx, 1, 0)
+                at(dx, 0, 1)
+                at(dx, 0, 0)
+
+            at(0, 1, 1)
+            at(0, 1, 0)
+            at(0, 0, 1)
+
+    def greet(peer):
+        pl.semaphore_signal(barrier, inc=1, device_id=peer, device_id_type=MESH)
+
+    fan("col", greet)
+    fan("row", greet)
 
     loads = [
         pltpu.make_async_copy(src, dst, in_sem.at[n])
@@ -103,6 +141,8 @@
     left = lane < 64
     masks = head_masks(sub, lane)
 
+    gz16[...] = jnp.zeros_like(gz16)
+
     live4 = jnp.zeros((4, 128), F32)
     sub4 = lax.broadcasted_iota(jnp.int32, (4, 128), 0)
     first = r * TILE + c * 4
@@ -128,9 +168,8 @@
 
     pack_block(q_v, qp_v, gs_v, gp_v, 64, live4, qsend)
     pack_block(k_v, kp_v, v_v, vp_v, 80, jnp.ones((4, 128), F32), ksend)
-    gz32[...] = jnp.zeros_like(gz32)
     for h in range(H):
-        gz32[pl.ds(h, 4, stride=HP), :] = gz_v[:, 128 * h : 128 * h + 128].astype(F32) * live4
+        gz32[pl.ds(h, 4, stride=H), :] = gz_v[:, 128 * h : 128 * h + 128].astype(F32) * live4
     gzsend[...] = gz32[...].astype(BF16)
     qg[c] = qsend[...]
     kg[r] = ksend[...]
@@ -143,8 +182,7 @@
         cb = jnp.where(sub == h, cb_s[h], cb)
     ps = W_LOGIT * ps * W_POINT / 2.0
     ps_lane = [jnp.sum(masks[t] * ps, 0, keepdims=True) for t in (2, 3)]
-    bw_pad = jnp.concatenate((bw_v[...], jnp.zeros((128, 128 - H), F32)), 1)
-    bw_t = jnp.transpose(bw_pad)[0:HP, :]
+    bw_t = jnp.concatenate((bw_v[...], jnp.zeros((HP - H, 128), F32)), 0)
     bw_high, bw_low = split(bw_t)
     wb_high, wb_low = split(W_LOGIT * bw_t)
     col_at = c * TILE
@@ -166,7 +204,9 @@
         high, low = split(pair_v[pl.ds(256 * t, 256), :])
         both = jnp.concatenate((high, low), 1)
         pp[pl.ds(256 * t, 256), :] = both
-        res = nt(bias_lhs, both)
+        both_t = jnp.transpose(both)
+        ppt[t] = both_t
+        res = nn(bias_lhs, both_t)
         res = res[0:HP] + res[HP : 2 * HP]
         for a in range(2):
             at = r * TILE + 4 * t + 2 * a
@@ -181,32 +221,32 @@
     def spread(src, dst, axis, n):
         me = c if axis == "col" else r
 
-        @pl.loop(1, PEERS)
-        def _(s):
-            to = lax.rem(me + s, PEERS)
+        def act(peer):
             pltpu.make_async_remote_copy(
                 src_ref=src,
                 dst_ref=dst.at[me],
                 send_sem=send_sem.at[n],
                 recv_sem=recv_sem.at[n],
-                device_id=(r, to) if axis == "col" else (to, c),
+                device_id=peer,
                 device_id_type=MESH,
             ).start()
 
+        fan(axis, act)
+
     def scatter(src, dst, axis, n):
         me = c if axis == "col" else r
 
-        @pl.loop(1, PEERS)
-        def _(s):
-            to = lax.rem(me + s, PEERS)
+        def act(peer):
             pltpu.make_async_remote_copy(
-                src_ref=src.at[to],
+                src_ref=src.at[peer[1] if axis == "col" else peer[0]],
                 dst_ref=dst.at[me],
                 send_sem=send_sem.at[n],
                 recv_sem=recv_sem.at[n],
-                device_id=(r, to) if axis == "col" else (to, c),
+                device_id=peer,
                 device_id_type=MESH,
             ).start()
+
+        fan(axis, act)
 
     def wait_recv(dst, n):
         part = dst.at[pl.ds(0, PEERS - 1)]
@@ -228,24 +268,23 @@
 
     wait_recv(kg, 1)
     assemble(kg, kf)
-    kb = kf[...].astype(BF16)
-    kdup[0:TILE, :] = kb
-    kdup[TILE : 2 * TILE, :] = kb
+    k_t = jnp.transpose(kf[...])
+    k_t = jnp.concatenate((k_t, k_t), 1)
+    kdup[...] = k_t.astype(BF16)
     for h in range(H):
         for t in range(4):
             kbd[TILE * h : TILE * h + TILE, 128 * t : 128 * t + 128] = (
                 kf[:, 128 * t : 128 * t + 128] * masks[t][h : h + 1, :]
             ).astype(BF16)
-    kp_sq_high, kp_sq_low = split(kf[:, 256:512] * kf[:, 256:512])
     point_mask = jnp.concatenate((masks[2], masks[3]), 1)
     point_mask16 = point_mask.astype(BF16)
-    k_sq = nt(point_mask16, kp_sq_high) + nt(point_mask16, kp_sq_low)
-    k_sq = jnp.concatenate((k_sq, k_sq), 1)
+    square_high, square_low = split(k_t[256:512] * k_t[256:512])
+    k_sq = nn(point_mask16, square_high) + nn(point_mask16, square_low)
 
     wait_recv(qg, 0)
     assemble(qg, qf)
 
-    @pl.loop(0, 8)
+    @pl.loop(0, 8, unroll=8)
     def _(b):
         eight = qf[pl.ds(pl.multiple_of(8 * b, 8), 8), :]
         for p in range(4):
@@ -261,18 +300,26 @@
                 sums.append(jnp.sum(square, 1, keepdims=True))
             qsq[rows, :] = jnp.where(left, sums[0], sums[1])
 
+    half_of = lax.broadcasted_iota(jnp.int32, (256, 128), 0) % 128 // 64
+    parity = lax.broadcasted_iota(jnp.int32, (256, 128), 1) % 2
+    half_ones = (half_of == parity).astype(F32).astype(BF16)
+
+    def half_sums(x):
+        return nn(jnp.concatenate(split(x), 1), half_ones)
+
+    lane_pair = lane // 2
     stats[...] = jnp.zeros_like(stats)
     lane3 = lax.broadcasted_iota(jnp.int32, (8, HP, 128), 2)
     left3 = lane3 < 64
 
-    @pl.loop(0, 4)
+    @pl.loop(0, 4, unroll=4)
     def _(b):
         rows = pl.ds(128 * b, 128)
         parts = []
         for k0, k1 in ((0, 256), (256, 512), (512, 1024)):
-            even = nt(qbd[0, rows, k0:k1], kdup[:, k0:k1]).reshape(8, HP, 128)
-            odd = nt(qbd[1, rows, k0:k1], kdup[:, k0:k1]).reshape(8, HP, 128)
-            parts.append(jnp.where(left3, even, odd))
+            both = nn(jnp.concatenate((qbd[0, rows, k0:k1], qbd[1, rows, k0:k1]), 0), kdup[k0:k1, :])
+            both = both.reshape(2, 8, HP, 128)
+            parts.append(jnp.where(left3, both[0], both[1]))
         dprob[rows, :] = parts[2].reshape(128, 128)
         distance = qsq[rows, :].reshape(8, HP, 128) + k_sq - 2.0 * parts[1]
         logits = base[rows, :].reshape(8, HP, 128) + SCALE_Q * parts[0] - ps * distance
@@ -280,35 +327,42 @@
         max0 = jnp.max(jnp.where(left3, logits, NEG_FILL), 2, keepdims=True)
         max1 = jnp.max(jnp.where(left3, NEG_FILL, logits), 2, keepdims=True)
         e = jnp.exp(logits - jnp.where(left3, max0, max1)) * live_k
-        sum0 = jnp.sum(jnp.where(left3, e, 0.0), 2, keepdims=True)
-        sum1 = jnp.sum(jnp.where(left3, 0.0, e), 2, keepdims=True)
-        expo[rows, :] = e.reshape(128, 128)
+        e = e.reshape(128, 128)
+        expo[rows, :] = e
+        sums = half_sums(e)
         acc_m, acc_s = stats[0], stats[1]
         for i in range(8):
             at = 16 * b + 2 * i
             acc_m = jnp.where(lane == at, max0[i], jnp.where(lane == at + 1, max1[i], acc_m))
-            acc_s = jnp.where(lane == at, sum0[i], jnp.where(lane == at + 1, sum1[i], acc_s))
+            acc_s = jnp.where(lane_pair == 8 * b + i, sums[HP * i : HP * i + HP], acc_s)
         stats[0] = acc_m
         stats[1] = acc_s
 
     wait_recv(gzg, 2)
 
-    @pl.loop(0, 16)
+    gz12[...] = gzg[...].astype(F32).reshape(PEERS * 4 * H, 128)
+
+    @pl.loop(0, PEERS, unroll=PEERS)
     def _(t):
-        gz = gzg[t]
-        res = nt(jnp.concatenate((gz, gz), 1), pp[pl.ds(256 * t, 256), :])
-        acc = stats[2]
+        for i in range(4):
+            gz16[pl.ds(64 * t + HP * i, H), :] = gz12[pl.ds(48 * t + H * i, H), :]
+
+    gzp[...] = gz16[...].astype(BF16).reshape(PEERS, 4 * HP, 128)
+
+    @pl.loop(0, 16, unroll=16)
+    def _(t):
+        gz = gzp[t]
+        res = nn(jnp.concatenate((gz, gz), 1), ppt[t])
         for a in range(2):
             rows = pl.ds(32 * t + 16 * a, 16)
             tile = res[32 * a : 32 * a + 32, 128 * a : 128 * a + 128]
-            value = dprob[rows, :] + jnp.where(left, tile[0:16], tile[16:32])
-            dprob[rows, :] = value
-            weighted = expo[rows, :] * value
-            sum0 = jnp.sum(jnp.where(left, weighted, 0.0), 1, keepdims=True)
-            sum1 = jnp.sum(jnp.where(left, 0.0, weighted), 1, keepdims=True)
-            at = 4 * t + 2 * a
-            acc = jnp.where(lane == at, sum0, jnp.where(lane == at + 1, sum1, acc))
-        stats[2] = acc
+            dprob[rows, :] = dprob[rows, :] + jnp.where(left, tile[0:16], tile[16:32])
+
+    sums = half_sums(expo[...] * dprob[...])
+    acc = jnp.zeros((HP, 128), F32)
+    for p in range(32):
+        acc = jnp.where(lane_pair == p, sums[HP * p : HP * p + HP], acc)
+    stats[2] = acc
 
     row_max, row_sum = stats[0], stats[1]
     any_live = row_sum > 0
@@ -332,7 +386,7 @@
     stats[0] = jnp.exp(row_max - top) / total
     stats[1] = dsum / total
 
-    @pl.loop(0, 8)
+    @pl.loop(0, 8, unroll=8)
     def _(b):
         scale = pltpu.roll(stats[0], lax.rem(128 - 8 * b, 128), 1)
         mean_all = pltpu.roll(stats[1], lax.rem(128 - 8 * b, 128), 1)
@@ -359,7 +413,7 @@
         )
         return acc + nn(lhs, pp[pl.ds(256 * t, 256), :])
 
-    w_all = lax.fori_loop(0, 16, weight_step, jnp.zeros((2 * HP, 256), F32))
+    w_all = lax.fori_loop(0, 16, weight_step, jnp.zeros((2 * HP, 256), F32), unroll=16)
     w_all = w_all[:, 0:128] + w_all[:, 128:256]
     w_send[...] = W_LOGIT * (w_all[0:HP] + w_all[HP : 2 * HP])
     w_row[r] = w_send[...]
@@ -426,9 +480,9 @@
     ]
     for n in range(4):
 
-        @pl.loop(4 * n, 4 * n + 4)
+        @pl.loop(4 * n, 4 * n + 4, unroll=4)
         def _(t):
-            gz = gzg[t]
+            gz = gzp[t]
             for a in range(2):
                 rows = pl.ds(32 * t + 16 * a, 16)
                 p = prob[rows, :]
@@ -448,39 +502,74 @@
 
         writes[n].start()
 
+    small = [
+        pltpu.make_async_copy(src, dst, out_sem.at[4 + n])
+        for n, (src, dst) in enumerate(
+            (
+                (gq_v, gq_out), (gqp_v, gqp_out), (gk_v, gk_out), (gkp_v, gkp_out), (gv_v, gv_out),
+                (gvp_v, gvp_out), (gbw_v, gbw_out),
+            )
+        )
+    ]
     wait_recv(kr, 5)
     ksum = kr[0]
     for s in range(1, PEERS):
         ksum = ksum + kr[s]
-    gk_out[:, 0:128] = ksum[0:4]
-    gk_out[:, 128:192] = ksum[4:8, 0:64]
-    gkp_out[:, 0:128] = ksum[8:12]
-    gkp_out[:, 128:144] = ksum[12:16, 0:16]
-    gv_out[:, 0:128] = ksum[16:20]
-    gv_out[:, 128:192] = ksum[28:32, 0:64]
-    gvp_out[:, 0:128] = ksum[20:24]
-    gvp_out[:, 128:256] = ksum[24:28]
-    gvp_out[:, 256:288] = ksum[28:32, 64:96]
+    gk_v[:, 0:128] = ksum[0:4]
+    gk_v[:, 128:192] = ksum[4:8, 0:64]
+    gkp_v[:, 0:128] = ksum[8:12]
+    gkp_v[:, 128:144] = ksum[12:16, 0:16]
+    gv_v[:, 0:128] = ksum[16:20]
+    gv_v[:, 128:192] = ksum[28:32, 0:64]
+    gvp_v[:, 0:128] = ksum[20:24]
+    gvp_v[:, 128:256] = ksum[24:28]
+    gvp_v[:, 256:288] = ksum[28:32, 64:96]
+    for n in range(2, 6):
+        small[n].start()
     wait_recv(qr, 6)
     qsum = qr[0]
     for s in range(1, PEERS):
         qsum = qsum + qr[s]
-    gq_out[:, 0:128] = qsum[0:4]
-    gq_out[:, 128:192] = qsum[4:8, 0:64]
-    gqp_out[:, 0:128] = qsum[8:12]
-    gqp_out[:, 128:144] = qsum[12:16, 0:16]
+    gq_v[:, 0:128] = qsum[0:4]
+    gq_v[:, 128:192] = qsum[4:8, 0:64]
+    gqp_v[:, 0:128] = qsum[8:12]
+    gqp_v[:, 128:144] = qsum[12:16, 0:16]
+
+    small[0].start()
+    small[1].start()
 
     wait_recv(w_col, 7)
     w_sum = w_col[0]
     for s in range(1, PEERS):
         w_sum = w_sum + w_col[s]
-    w_full = jnp.concatenate((w_sum, jnp.zeros((128 - HP, 128), F32)), 0)
-    gbw_out[...] = jnp.transpose(w_full)[:, 0:H]
+    gbw_v[...] = w_sum[0:H]
+    small[6].start()
 
     for n, dst in enumerate((qg, kg, gzg, stat_g, w_row, kr, qr, w_col)):
         wait_send(dst, n)
-    for write in writes:
+    for write in writes + small:
         write.wait()
+
+
+def finish(*refs):
+    srcs, dsts, held, sem = refs[0:8], refs[8:16], refs[16:24], refs[24]
+    rows = 4096 // CHUNKS
+    parts = [(n, None) for n in range(8) if n != 6] + [(6, pl.ds(rows * k, rows)) for k in range(CHUNKS)]
+    moves = []
+    for at, (n, part) in enumerate(parts):
+        src, mid, dst = srcs[n], held[n], dsts[n]
+        if part is not None:
+            src, mid, dst = src.at[part], mid.at[part], dst.at[part]
+        moves.append(
+            (pltpu.make_async_copy(src, mid, sem.at[0, at]), pltpu.make_async_copy(mid, dst, sem.at[1, at]))
+        )
+    for load, _ in moves:
+        load.start()
+    for load, store in moves:
+        load.wait()
+        store.start()
+    for _, store in moves:
+        store.wait()
 
 
 def on_device(
@@ -488,51 +577,59 @@
     head_weight, chain_bias, chain_ids, live_mask, cot_scalar, cot_points, cot_pair,
 ):
     any_spec = pl.BlockSpec(memory_space=pl.ANY)
-    vmem_spec = pl.BlockSpec(memory_space=pltpu.VMEM)
 
     def vm(*shape, kind=F32):
         return pltpu.VMEM(shape, kind)
 
     scratch = [
         vm(4, 192, kind=BF16), vm(4, 144, kind=BF16), vm(4, 192, kind=BF16), vm(4, 144, kind=BF16),
-        vm(4, 192, kind=BF16), vm(4, 288, kind=BF16), vm(4096, 128), vm(128, H),
+        vm(4, 192, kind=BF16), vm(4, 288, kind=BF16), vm(4096, 128), vm(H, 128),
         pltpu.SMEM((H,), F32), pltpu.SMEM((H,), F32),
         pltpu.SMEM((8, 128), jnp.int32), pltpu.SMEM((8, 128), jnp.int32),
         vm(8, 128, kind=jnp.int32), vm(8, 128, kind=jnp.int32),
         vm(4, 192, kind=BF16), vm(4, 288, kind=BF16), vm(4, 1536, kind=BF16),
-        vm(32, 128), vm(64, 128), vm(32, 128, kind=BF16), vm(32, 128, kind=BF16), vm(64, 128, kind=BF16),
-        vm(PEERS, 32, 128, kind=BF16), vm(PEERS, 32, 128, kind=BF16), vm(PEERS, 64, 128, kind=BF16),
-        vm(PEERS, 32, 128),
-        vm(TILE, 1024), vm(TILE, 1024), vm(2 * TILE, 1024, kind=BF16), vm(2, 512, 1024, kind=BF16),
-        vm(H * TILE, 512, kind=BF16), vm(4096, 256, kind=BF16), vm(512, 128), vm(512, 128), vm(512, 128),
+        vm(32, 128), vm(4 * H, 128), vm(32, 128, kind=BF16), vm(32, 128, kind=BF16), vm(4 * H, 128, kind=BF16),
+        vm(PEERS, 32, 128, kind=BF16), vm(PEERS, 32, 128, kind=BF16), vm(PEERS, 4 * H, 128, kind=BF16),
+        vm(PEERS, 32, 128), vm(PEERS * 4 * H, 128), vm(PEERS * 4 * HP, 128), vm(PEERS, 4 * HP, 128, kind=BF16),
+        vm(TILE, 1024), vm(TILE, 1024), vm(1024, 128, kind=BF16), vm(2, 512, 1024, kind=BF16),
+        vm(H * TILE, 512, kind=BF16), vm(4096, 256, kind=BF16), vm(16, 256, 256, kind=BF16), vm(512, 128), vm(512, 128), vm(512, 128),
         vm(512, 128), vm(512, 128), vm(512, 128), vm(512, 128, kind=BF16),
         vm(3, HP, 128), vm(HP, 128), vm(PEERS, HP, 128), vm(HP, 128), vm(PEERS, HP, 128), vm(HP, 128),
         vm(PEERS, HP, 128),
         vm(TILE, 1024), vm(PEERS, 32, 128), vm(PEERS, 32, 128), vm(4, TILE, 128), vm(PEERS, 16, 128),
         vm(PEERS, 16, 128),
-        pltpu.SemaphoreType.DMA((17,)), pltpu.SemaphoreType.DMA((4,)),
+        vm(4, 192), vm(4, 144), vm(4, 192), vm(4, 144), vm(4, 192), vm(4, 288), vm(H, 128),
+        pltpu.SemaphoreType.DMA((17,)), pltpu.SemaphoreType.DMA((11,)),
         pltpu.SemaphoreType.DMA((8,)), pltpu.SemaphoreType.DMA((8,)),
     ]
     out_shape = [
         jax.ShapeDtypeStruct(shape, F32)
-        for shape in ((4, 192), (4, 144), (4, 192), (4, 144), (4, 192), (4, 288), (4096, 128), (128, H))
+        for shape in ((4, 192), (4, 144), (4, 192), (4, 144), (4, 192), (4, 288), (4096, 128), (H, 128))
     ]
     out = pl.pallas_call(
         kernel,
         out_shape=out_shape,
         in_specs=[any_spec] * 15,
-        out_specs=[vmem_spec] * 6 + [any_spec, vmem_spec],
+        out_specs=[any_spec] * 8,
         scratch_shapes=scratch,
         compiler_params=pltpu.CompilerParams(
-            collective_id=0, has_side_effects=True, vmem_limit_bytes=40 * 2**20
+            collective_id=0, has_side_effects=True, vmem_limit_bytes=VMEM_LIMIT
         ),
         cost_estimate=pl.CostEstimate(flops=10**9, bytes_accessed=5 * 2**20, transcendentals=10**5),
     )(
         queries, query_points, key_feats, key_points, values, value_points,
-        pair_rep.reshape(4096, 128), bias_weight, head_weight, chain_bias,
+        pair_rep.reshape(4096, 128), bias_weight.T, head_weight, chain_bias,
         chain_ids.reshape(8, 128), live_mask.reshape(8, 128), cot_scalar, cot_points, cot_pair,
     )
-    return (*out[:6], out[6].reshape(TILE, TILE, 128), out[7])
+    out = pl.pallas_call(
+        finish,
+        out_shape=out_shape,
+        in_specs=[any_spec] * 8,
+        out_specs=[any_spec] * 8,
+        scratch_shapes=[vm(*shape.shape) for shape in out_shape] + [pltpu.SemaphoreType.DMA((2, 7 + CHUNKS))],
+        compiler_params=pltpu.CompilerParams(vmem_limit_bytes=VMEM_LIMIT),
+    )(*out)
+    return (*out[:6], out[6].reshape(TILE, TILE, 128), out[7].T)
 
 
 def solution(mesh):

time: 67.4 us -> 44.7 us (0.66)
  local copies, waits for them, and re-layouts: 16.8 us -> 0 us
  Pallas kernels: 49.5 us -> 43.9 us
    unnamed x37 -> x0, local copies, waits for them, and re-layouts: 16.8 us -> none
    pallas_call x1, Pallas kernels: 49.5 us -> 41.4 us  [on_device(): pl.pallas_call(kernel, out_shape=out_shape, in_specs=[any_spec] * 15, out...]
    pallas_call x0 -> x1, Pallas kernels: none -> 2.58 us  [on_device(): pl.pallas_call(finish, out_shape=out_shape, in_specs=[any_spec] * 8, out_...]
where the time goes in v2:
time: 44.7 us; the launch traced here: 44.6 us
  Pallas kernels  43.9 us (98%)
  between operations  0.65 us (1%)
    pallas_call x1, Pallas kernels, on_device(): pl.pallas_call(kernel, out_shape=out_shape, in_specs=[any_spec] * 15, out...  41.4 us
    pallas_call x1, Pallas kernels, on_device(): pl.pallas_call(finish, out_shape=out_shape, in_specs=[any_spec] * 8, out_...  2.58 us

profile of v2, /device:TPU:1, one launch (start us, length us, event | category | flops | bytes accessed | tf_op | source)
XLA Modules:
  0.0 44.6 jit_solution(8641533270237835146)
XLA Ops:
  0.6 41.4 %shard_map.206 = (f32[4,192]{1,0:T(4,128)}, f32[4,144]{1,0:T(4,128)}, f32[4,192]{1,0:T(4,128)}, f32[4,144]{1,0:T(4,128)}, f32[4,192]{1,0:T(4,128)}, /*index=5*/f...) custom-call(bf16[4,192]{1,0:T(4,128)(2,1)} %q_in.1, bf16[4,144]{1,0:T(4,128)(2,1)} %qp_in.1, bf16[4,192]{1,0:T(4,128)(2,1)} %k_in.1, ...), custom_call_target="tpu_custom_call" | custom-call | flops 1000000000 | bytes 5242880 | tf_op jit(solution)/shard_map/pallas_call | solution.py:609
  42.0 2.6 %shard_map.207 = (f32[4,192]{1,0:T(4,128)}, f32[4,144]{1,0:T(4,128)}, f32[4,192]{1,0:T(4,128)}, f32[4,144]{1,0:T(4,128)}, f32[4,192]{1,0:T(4,128)}, /*index=5*/f...) custom-call(f32[4,192]{1,0:T(4,128)} %get-tuple-element.24.refs_0_, f32[4,144]{1,0:T(4,128)} %get-tuple-element.25.refs_1_, ...), custom_call_target="tpu_custom_call" | custom-call | tf_op jit(solution)/shard_map/pallas_call | solution.py:624

commit v3 on v2

--- a/solution.py
+++ b/solution.py
@@ -15,8 +15,7 @@
 HP = 16
 TILE = 64
 PEERS = 16
-VMEM_LIMIT = 60 * 2**20
-CHUNKS = 8
+VMEM_LIMIT = 40 * 2**20
 W_LOGIT = math.sqrt(1.0 / 3.0)
 W_POINT = math.sqrt(2.0 / 36.0)
 SCALE_Q = W_LOGIT / 4.0
@@ -68,8 +67,7 @@
     qf, kf, kdup, qbd, kbd, pp, ppt, base, qsq, expo, dprob, prob, dsr, dlo,
     stats, stat_send, stat_g, w_send, w_row, w_mid, w_col,
     kres, kch, kr, qres, qch, qr,
-    gq_v, gqp_v, gk_v, gkp_v, gv_v, gvp_v, gbw_v,
-    in_sem, out_sem, send_sem, recv_sem,
+    in_sem, send_sem, recv_sem,
 ):
     r = lax.axis_index("row")
     c = lax.axis_index("col")
@@ -194,6 +192,50 @@
     chain_k = jnp.where(own, chain_k, pltpu.roll(chain_k, 64, 1))
     live_k = jnp.where(own, live_k, pltpu.roll(live_k, 64, 1))
 
+    pl.semaphore_wait(barrier, 2 * (PEERS - 1))
+
+    def spread(src, dst, axis, n):
+        me = c if axis == "col" else r
+
+        def act(peer):
+            pltpu.make_async_remote_copy(
+                src_ref=src,
+                dst_ref=dst.at[me],
+                send_sem=send_sem.at[n],
+                recv_sem=recv_sem.at[n],
+                device_id=peer,
+                device_id_type=MESH,
+            ).start()
+
+        fan(axis, act)
+
+    def scatter(src, dst, axis, n):
+        me = c if axis == "col" else r
+
+        def act(peer):
+            pltpu.make_async_remote_copy(
+                src_ref=src.at[peer[1] if axis == "col" else peer[0]],
+                dst_ref=dst.at[me],
+                send_sem=send_sem.at[n],
+                recv_sem=recv_sem.at[n],
+                device_id=peer,
+                device_id_type=MESH,
+            ).start()
+
+        fan(axis, act)
+
+    def wait_recv(dst, n):
+        part = dst.at[pl.ds(0, PEERS - 1)]
+        pltpu.make_async_copy(part, part, recv_sem.at[n]).wait()
+
+    def wait_send(dst, n):
+        part = dst.at[pl.ds(0, PEERS - 1)]
+        pltpu.make_async_copy(part, part, send_sem.at[n]).wait()
+
+    spread(qsend, qg, "col", 0)
+    spread(ksend, kg, "row", 1)
+    spread(gzsend, gzg, "col", 2)
+
     loads[0].wait()
     bias_lhs = jnp.concatenate(
         (jnp.concatenate((bw_high, bw_high), 1), jnp.concatenate((bw_low, bw_low), 1)), 0
@@ -215,50 +257,6 @@
             )
             same = (chain_q == chain_k).astype(F32)
             base[pl.ds(32 * t + 16 * a, 16), :] = W_LOGIT * (res[:, 128 * a : 128 * a + 128] + cb * same)
-
-    pl.semaphore_wait(barrier, 2 * (PEERS - 1))
-
-    def spread(src, dst, axis, n):
-        me = c if axis == "col" else r
-
-        def act(peer):
-            pltpu.make_async_remote_copy(
-                src_ref=src,
-                dst_ref=dst.at[me],
-                send_sem=send_sem.at[n],
-                recv_sem=recv_sem.at[n],
-                device_id=peer,
-                device_id_type=MESH,
-            ).start()
-
-        fan(axis, act)
-
-    def scatter(src, dst, axis, n):
-        me = c if axis == "col" else r
-
-        def act(peer):
-            pltpu.make_async_remote_copy(
-                src_ref=src.at[peer[1] if axis == "col" else peer[0]],
-                dst_ref=dst.at[me],
-                send_sem=send_sem.at[n],
-                recv_sem=recv_sem.at[n],
-                device_id=peer,
-                device_id_type=MESH,
-            ).start()
-
-        fan(axis, act)
-
-    def wait_recv(dst, n):
-        part = dst.at[pl.ds(0, PEERS - 1)]
-        pltpu.make_async_copy(part, part, recv_sem.at[n]).wait()
-
-    def wait_send(dst, n):
-        part = dst.at[pl.ds(0, PEERS - 1)]
-        pltpu.make_async_copy(part, part, send_sem.at[n]).wait()
-
-    spread(qsend, qg, "col", 0)
-    spread(ksend, kg, "row", 1)
-    spread(gzsend, gzg, "col", 2)
 
     def assemble(got, full):
         blk[...] = got[...].astype(F32)
@@ -472,104 +470,66 @@
     spread(w_mid, w_col, "col", 7)
 
     wb = jnp.concatenate((wb_high, wb_high, wb_low), 0)
-    writes = [
-        pltpu.make_async_copy(
-            pair_v.at[pl.ds(1024 * n, 1024)], gpair_out.at[pl.ds(1024 * n, 1024)], out_sem.at[n]
-        )
-        for n in range(4)
-    ]
-    for n in range(4):
-
-        @pl.loop(4 * n, 4 * n + 4, unroll=4)
-        def _(t):
-            gz = gzp[t]
-            for a in range(2):
-                rows = pl.ds(32 * t + 16 * a, 16)
-                p = prob[rows, :]
-                high = dsr[rows, :].astype(BF16)
-                lhs = jnp.concatenate(
-                    (
-                        jnp.where(left, p, 0.0).astype(BF16),
-                        jnp.where(left, 0.0, p).astype(BF16),
-                        high,
-                        dlo[rows, :],
-                        high,
-                    ),
-                    0,
-                )
-                rhs = jnp.concatenate((gz[32 * a : 32 * a + 32], wb), 0)
-                pair_v[pl.ds(256 * t + 128 * a, 128), :] = tn(lhs, rhs)
-
-        writes[n].start()
-
-    small = [
-        pltpu.make_async_copy(src, dst, out_sem.at[4 + n])
-        for n, (src, dst) in enumerate(
-            (
-                (gq_v, gq_out), (gqp_v, gqp_out), (gk_v, gk_out), (gkp_v, gkp_out), (gv_v, gv_out),
-                (gvp_v, gvp_out), (gbw_v, gbw_out),
+    @pl.loop(0, 16, unroll=16)
+    def _(t):
+        gz = gzp[t]
+        for a in range(2):
+            rows = pl.ds(32 * t + 16 * a, 16)
+            p = prob[rows, :]
+            high = dsr[rows, :].astype(BF16)
+            lhs = jnp.concatenate(
+                (
+                    jnp.where(left, p, 0.0).astype(BF16),
+                    jnp.where(left, 0.0, p).astype(BF16),
+                    high,
+                    dlo[rows, :],
+                    high,
+                ),
+                0,
             )
-        )
-    ]
+            rhs = jnp.concatenate((gz[32 * a : 32 * a + 32], wb), 0)
+            gpair_out[pl.ds(256 * t + 128 * a, 128), :] = tn(lhs, rhs)
+
     wait_recv(kr, 5)
     ksum = kr[0]
     for s in range(1, PEERS):
         ksum = ksum + kr[s]
-    gk_v[:, 0:128] = ksum[0:4]
-    gk_v[:, 128:192] = ksum[4:8, 0:64]
-    gkp_v[:, 0:128] = ksum[8:12]
-    gkp_v[:, 128:144] = ksum[12:16, 0:16]
-    gv_v[:, 0:128] = ksum[16:20]
-    gv_v[:, 128:192] = ksum[28:32, 0:64]
-    gvp_v[:, 0:128] = ksum[20:24]
-    gvp_v[:, 128:256] = ksum[24:28]
-    gvp_v[:, 256:288] = ksum[28:32, 64:96]
-    for n in range(2, 6):
-        small[n].start()
+    gk_out[:, 0:128] = ksum[0:4]
+    gk_out[:, 128:192] = ksum[4:8, 0:64]
+    gkp_out[:, 0:128] = ksum[8:12]
+    gkp_out[:, 128:144] = ksum[12:16, 0:16]
+    gv_out[:, 0:128] = ksum[16:20]
+    gv_out[:, 128:192] = ksum[28:32, 0:64]
+    gvp_out[:, 0:128] = ksum[20:24]
+    gvp_out[:, 128:256] = ksum[24:28]
+    gvp_out[:, 256:288] = ksum[28:32, 64:96]
     wait_recv(qr, 6)
     qsum = qr[0]
     for s in range(1, PEERS):
         qsum = qsum + qr[s]
-    gq_v[:, 0:128] = qsum[0:4]
-    gq_v[:, 128:192] = qsum[4:8, 0:64]
-    gqp_v[:, 0:128] = qsum[8:12]
-    gqp_v[:, 128:144] = qsum[12:16, 0:16]
-
-    small[0].start()
-    small[1].start()
+    gq_out[:, 0:128] = qsum[0:4]
+    gq_out[:, 128:192] = qsum[4:8, 0:64]
+    gqp_out[:, 0:128] = qsum[8:12]
+    gqp_out[:, 128:144] = qsum[12:16, 0:16]
+
 
     wait_recv(w_col, 7)
     w_sum = w_col[0]
     for s in range(1, PEERS):
         w_sum = w_sum + w_col[s]
-    gbw_v[...] = w_sum[0:H]
-    small[6].start()
+    gbw_out[...] = w_sum[0:H]
 
     for n, dst in enumerate((qg, kg, gzg, stat_g, w_row, kr, qr, w_col)):
         wait_send(dst, n)
-    for write in writes + small:
-        write.wait()
 
 
 def finish(*refs):
-    srcs, dsts, held, sem = refs[0:8], refs[8:16], refs[16:24], refs[24]
-    rows = 4096 // CHUNKS
-    parts = [(n, None) for n in range(8) if n != 6] + [(6, pl.ds(rows * k, rows)) for k in range(CHUNKS)]
-    moves = []
-    for at, (n, part) in enumerate(parts):
-        src, mid, dst = srcs[n], held[n], dsts[n]
-        if part is not None:
-            src, mid, dst = src.at[part], mid.at[part], dst.at[part]
-        moves.append(
-            (pltpu.make_async_copy(src, mid, sem.at[0, at]), pltpu.make_async_copy(mid, dst, sem.at[1, at]))
-        )
-    for load, _ in moves:
-        load.start()
-    for load, store in moves:
-        load.wait()
-        store.start()
-    for _, store in moves:
-        store.wait()
+    sem = refs[-1]
+    copies = [pltpu.make_async_copy(refs[n], refs[8 + n], sem.at[n]) for n in range(8)]
+    for copy in copies:
+        copy.start()
+    for copy in copies:
+        copy.wait()
 
 
 def on_device(
@@ -577,6 +537,7 @@
     head_weight, chain_bias, chain_ids, live_mask, cot_scalar, cot_points, cot_pair,
 ):
     any_spec = pl.BlockSpec(memory_space=pl.ANY)
+    vmem_spec = pl.BlockSpec(memory_space=pltpu.VMEM)
 
     def vm(*shape, kind=F32):
         return pltpu.VMEM(shape, kind)
@@ -598,8 +559,7 @@
         vm(PEERS, HP, 128),
         vm(TILE, 1024), vm(PEERS, 32, 128), vm(PEERS, 32, 128), vm(4, TILE, 128), vm(PEERS, 16, 128),
         vm(PEERS, 16, 128),
-        vm(4, 192), vm(4, 144), vm(4, 192), vm(4, 144), vm(4, 192), vm(4, 288), vm(H, 128),
-        pltpu.SemaphoreType.DMA((17,)), pltpu.SemaphoreType.DMA((11,)),
+        pltpu.SemaphoreType.DMA((17,)),
         pltpu.SemaphoreType.DMA((8,)), pltpu.SemaphoreType.DMA((8,)),
     ]
     out_shape = [
@@ -608,26 +568,26 @@
     ]
     out = pl.pallas_call(
         kernel,
-        out_shape=out_shape,
+        out_shape=[pltpu.VMEM(shape.shape, F32) for shape in out_shape],
         in_specs=[any_spec] * 15,
-        out_specs=[any_spec] * 8,
+        out_specs=[vmem_spec] * 8,
         scratch_shapes=scratch,
         compiler_params=pltpu.CompilerParams(
             collective_id=0, has_side_effects=True, vmem_limit_bytes=VMEM_LIMIT
         ),
         cost_estimate=pl.CostEstimate(flops=10**9, bytes_accessed=5 * 2**20, transcendentals=10**5),
-    )(
+    )(*(pltpu.with_memory_space_constraint(x, pltpu.HBM) for x in (
         queries, query_points, key_feats, key_points, values, value_points,
         pair_rep.reshape(4096, 128), bias_weight.T, head_weight, chain_bias,
         chain_ids.reshape(8, 128), live_mask.reshape(8, 128), cot_scalar, cot_points, cot_pair,
-    )
+    )))
     out = pl.pallas_call(
         finish,
         out_shape=out_shape,
-        in_specs=[any_spec] * 8,
+        in_specs=[vmem_spec] * 8,
         out_specs=[any_spec] * 8,
-        scratch_shapes=[vm(*shape.shape) for shape in out_shape] + [pltpu.SemaphoreType.DMA((2, 7 + CHUNKS))],
-        compiler_params=pltpu.CompilerParams(vmem_limit_bytes=VMEM_LIMIT),
+        scratch_shapes=[pltpu.SemaphoreType.DMA((8,))],
+        compiler_params=pltpu.CompilerParams(vmem_limit_bytes=2**20),
     )(*out)
     return (*out[:6], out[6].reshape(TILE, TILE, 128), out[7].T)
 

time: 44.7 us -> 40 us (0.89)
  Pallas kernels: 43.9 us -> 39.3 us
    pallas_call x2, Pallas kernels: 43.9 us -> 39.3 us  [the longest x1 37.8 us: on_device(): pl.pallas_call(kernel, out_shape=[pltpu.VMEM(shape.shape, F32) for shape...]
where the time goes in v3:
time: 40 us; the launch traced here: 39.9 us
  Pallas kernels  39.3 us (98%)
  between operations  0.65 us (2%)
    pallas_call x1, Pallas kernels, on_device(): pl.pallas_call(kernel, out_shape=[pltpu.VMEM(shape.shape, F32) for shape...  37.8 us
    pallas_call x1, Pallas kernels, on_device(): pl.pallas_call(finish, out_shape=out_shape, in_specs=[vmem_spec] * 8, out...  1.42 us

profile of v3, /device:TPU:1, one launch (start us, length us, event | category | flops | bytes accessed | tf_op | source)
XLA Modules:
  0.0 39.9 jit_solution(5848009491236127616)
XLA Ops:
  0.6 37.8 %shard_map.206 = (f32[4,192]{1,0:T(4,128)S(1)}, f32[4,144]{1,0:T(4,128)S(1)}, f32[4,192]{1,0:T(4,128)S(1)}, f32[4,144]{1,0:T(4,128)S(1)}, f32[4,192]{1,0:T(4,128...) custom-call(bf16[4,192]{1,0:T(4,128)(2,1)} %q_in.1, bf16[4,144]{1,0:T(4,128)(2,1)} %qp_in.1, ...), custom_call_target="tpu_custom_call" | custom-call | flops 1000000000 | bytes 5242880 | tf_op jit(solution)/shard_map/pallas_call | solution.py:569
  38.5 1.4 %shard_map.207 = (f32[4,192]{1,0:T(4,128)}, f32[4,144]{1,0:T(4,128)}, f32[4,192]{1,0:T(4,128)}, f32[4,144]{1,0:T(4,128)}, f32[4,192]{1,0:T(4,128)}, /*index=5*/f...) custom-call(f32[4,192]{1,0:T(4,128)S(1)} %get-tuple-element.24.refs_0_, f32[4,144]{1,0:T(4,128)S(1)} %get-tuple-element.25.refs_1_, ...), custom_call_target="tpu_custom_call" | custom-call | tf_op jit(solution)/shard_map/pallas_call | solution.py:584

commit v4 on v3

--- a/solution.py
+++ b/solution.py
@@ -16,6 +16,7 @@
 TILE = 64
 PEERS = 16
 VMEM_LIMIT = 40 * 2**20
+PIECES = 8
 W_LOGIT = math.sqrt(1.0 / 3.0)
 W_POINT = math.sqrt(2.0 / 36.0)
 SCALE_Q = W_LOGIT / 4.0
@@ -64,7 +65,7 @@
     q_v, qp_v, k_v, kp_v, v_v, vp_v, pair_v, bw_v, hw_s, cb_s, chain_s, live_s, chain_v, live_v,
     gs_v, gp_v, gz_v,
     pack, gz32, qsend, ksend, gzsend, qg, kg, gzg, blk, gz12, gz16, gzp,
-    qf, kf, kdup, qbd, kbd, pp, ppt, base, qsq, expo, dprob, prob, dsr, dlo,
+    qf, kf, kdup, qbd, kbd, pp, ppt, sums_xy, base, qsq, expo, dprob, prob, dsr, dlo,
     stats, stat_send, stat_g, w_send, w_row, w_mid, w_col,
     kres, kch, kr, qres, qch, qr,
     in_sem, send_sem, recv_sem,
@@ -81,16 +82,16 @@
                 dz = 4 + (1 - 2 * lax.rem(j, 2)) * ((j + 1) // 2)
                 act((r, lax.rem(y + dy, 2) * 8 + lax.rem(z + dz, 8)))
 
-            @pl.loop(0, 3)
+            @pl.loop(0, 3, unroll=3)
             def _(j):
                 at(1, j)
 
-            @pl.loop(3, 8)
+            @pl.loop(3, 8, unroll=5)
             def _(j):
                 at(1, j)
                 at(0, j - 3)
 
-            @pl.loop(5, 7)
+            @pl.loop(5, 7, unroll=2)
             def _(j):
                 at(0, j)
         else:
@@ -99,7 +100,7 @@
             def at(dx, dy, dc):
                 act((lax.rem(x + dx, 4) * 4 + lax.rem(y + dy, 2) * 2 + lax.rem(core + dc, 2), c))
 
-            @pl.loop(0, 3)
+            @pl.loop(0, 3, unroll=3)
             def _(m):
                 dx = 2 + (1 - 2 * lax.rem(m, 2)) * ((m + 1) // 2)
                 at(dx, 1, 1)
@@ -269,29 +270,24 @@
     k_t = jnp.transpose(kf[...])
     k_t = jnp.concatenate((k_t, k_t), 1)
     kdup[...] = k_t.astype(BF16)
-    for h in range(H):
-        for t in range(4):
-            kbd[TILE * h : TILE * h + TILE, 128 * t : 128 * t + 128] = (
-                kf[:, 128 * t : 128 * t + 128] * masks[t][h : h + 1, :]
-            ).astype(BF16)
     point_mask = jnp.concatenate((masks[2], masks[3]), 1)
     point_mask16 = point_mask.astype(BF16)
     square_high, square_low = split(k_t[256:512] * k_t[256:512])
     k_sq = nn(point_mask16, square_high) + nn(point_mask16, square_low)
 
     wait_recv(qg, 0)
-    assemble(qg, qf)
-
-    @pl.loop(0, 8, unroll=8)
-    def _(b):
-        eight = qf[pl.ds(pl.multiple_of(8 * b, 8), 8), :]
-        for p in range(4):
-            rows = pl.ds(64 * b + HP * p, HP)
+
+    @pl.loop(0, PEERS, unroll=PEERS)
+    def _(s):
+        got = qg[s].astype(F32)
+        for p in range(2):
+            rows = pl.ds(32 * s + HP * p, HP)
             sums = []
             for odd in range(2):
                 square = jnp.zeros((HP, 128), F32)
                 for t in range(8):
-                    value = eight[2 * p + odd : 2 * p + odd + 1, 128 * t : 128 * t + 128] * masks[t]
+                    at = 4 * t + 2 * p + odd
+                    value = got[at : at + 1, :] * masks[t]
                     qbd[odd, rows, 128 * t : 128 * t + 128] = value.astype(BF16)
                     if t in (2, 3):
                         square = square + value * value
@@ -370,6 +366,26 @@
     stat_send[...] = jnp.where(left, lse, pltpu.roll(mean, 64, 1))
     stat_g[c] = stat_send[...]
     spread(stat_send, stat_g, "col", 3)
+    assemble(qg, qf)
+    for h in range(H):
+        for t in range(4):
+            kbd[TILE * h : TILE * h + TILE, 128 * t : 128 * t + 128] = (
+                kf[:, 128 * t : 128 * t + 128] * masks[t][h : h + 1, :]
+            ).astype(BF16)
+
+    @pl.loop(0, 32, unroll=8)
+    def _(p):
+        rows = pl.ds(pl.multiple_of(HP * p, HP), HP)
+        e = expo[rows, :]
+        terms = []
+        for side in (left, jnp.logical_not(left)):
+            own = jnp.where(side, e, 0.0)
+            terms += [*split(own * dprob[rows, :]), *split(own)]
+        res = nn(jnp.concatenate(terms, 0), pp[pl.ds(pl.multiple_of(128 * p, 128), 128), :])
+        res = res[:, 0:128] + res[:, 128:256]
+        for n in range(4):
+            sums_xy[p, n] = res[32 * n : 32 * n + 16] + res[32 * n + 16 : 32 * n + 32]
+
     wait_recv(stat_g, 3)
     top = stat_g[0]
     for s in range(1, PEERS):
@@ -381,8 +397,24 @@
         weight = jnp.exp(got - top)
         total = total + weight
         dsum = dsum + weight * pltpu.roll(got, 64, 1)
-    stats[0] = jnp.exp(row_max - top) / total
-    stats[1] = dsum / total
+    scales = jnp.exp(row_max - top) / total
+    means = dsum / total
+    stats[0] = scales
+    stats[1] = means
+
+    shifts = scales * means
+    w_parts = []
+    for p in range(32):
+        part = jnp.zeros((HP, 128), F32)
+        for odd in range(2):
+            i = 2 * p + odd
+            part = part + scales[:, i : i + 1] * sums_xy[p, 2 * odd] - shifts[:, i : i + 1] * sums_xy[p, 2 * odd + 1]
+        w_parts.append(part)
+    while len(w_parts) > 1:
+        w_parts = [one + two for one, two in zip(w_parts[0::2], w_parts[1::2])]
+    w_send[...] = W_LOGIT * w_parts[0]
+    w_row[r] = w_send[...]
+    spread(w_send, w_row, "row", 4)
 
     @pl.loop(0, 8, unroll=8)
     def _(b):
@@ -398,24 +430,6 @@
             prob[rows, :] = p.astype(BF16).astype(F32)
             dsr[rows, :] = high.astype(F32)
             dlo[rows, :] = low
-
-    def weight_step(t, acc):
-        high = dsr[pl.ds(32 * t, 32), :].astype(BF16)
-        low = dlo[pl.ds(32 * t, 32), :]
-        lhs = jnp.concatenate(
-            (
-                jnp.concatenate((high[0:16], high[16:32]), 1),
-                jnp.concatenate((low[0:16], low[16:32]), 1),
-            ),
-            0,
-        )
-        return acc + nn(lhs, pp[pl.ds(256 * t, 256), :])
-
-    w_all = lax.fori_loop(0, 16, weight_step, jnp.zeros((2 * HP, 256), F32), unroll=16)
-    w_all = w_all[:, 0:128] + w_all[:, 128:256]
-    w_send[...] = W_LOGIT * (w_all[0:HP] + w_all[HP : 2 * HP])
-    w_row[r] = w_send[...]
-    spread(w_send, w_row, "row", 4)
 
     ds_t = jnp.transpose(dsr[...]).astype(BF16)
     prob_t = jnp.transpose(prob[...]).astype(BF16)
@@ -525,7 +539,10 @@
 
 def finish(*refs):
     sem = refs[-1]
-    copies = [pltpu.make_async_copy(refs[n], refs[8 + n], sem.at[n]) for n in range(8)]
+    rows = 4096 // PIECES
+    pairs = [(refs[6].at[pl.ds(rows * n, rows)], refs[14].at[pl.ds(rows * n, rows)]) for n in range(PIECES)]
+    pairs += [(refs[n], refs[8 + n]) for n in range(8) if n != 6]
+    copies = [pltpu.make_async_copy(src, dst, sem.at[n]) for n, (src, dst) in enumerate(pairs)]
     for copy in copies:
         copy.start()
     for copy in copies:
@@ -553,7 +570,7 @@
         vm(PEERS, 32, 128, kind=BF16), vm(PEERS, 32, 128, kind=BF16), vm(PEERS, 4 * H, 128, kind=BF16),
         vm(PEERS, 32, 128), vm(PEERS * 4 * H, 128), vm(PEERS * 4 * HP, 128), vm(PEERS, 4 * HP, 128, kind=BF16),
         vm(TILE, 1024), vm(TILE, 1024), vm(1024, 128, kind=BF16), vm(2, 512, 1024, kind=BF16),
-        vm(H * TILE, 512, kind=BF16), vm(4096, 256, kind=BF16), vm(16, 256, 256, kind=BF16), vm(512, 128), vm(512, 128), vm(512, 128),
+        vm(H * TILE, 512, kind=BF16), vm(4096, 256, kind=BF16), vm(16, 256, 256, kind=BF16), vm(32, 4, HP, 128), vm(512, 128), vm(512, 128), vm(512, 128),
         vm(512, 128), vm(512, 128), vm(512, 128), vm(512, 128, kind=BF16),
         vm(3, HP, 128), vm(HP, 128), vm(PEERS, HP, 128), vm(HP, 128), vm(PEERS, HP, 128), vm(HP, 128),
         vm(PEERS, HP, 128),
@@ -586,7 +603,7 @@
         out_shape=out_shape,
         in_specs=[vmem_spec] * 8,
         out_specs=[any_spec] * 8,
-        scratch_shapes=[pltpu.SemaphoreType.DMA((8,))],
+        scratch_shapes=[pltpu.SemaphoreType.DMA((7 + PIECES,))],
         compiler_params=pltpu.CompilerParams(vmem_limit_bytes=2**20),
     )(*out)
     return (*out[:6], out[6].reshape(TILE, TILE, 128), out[7].T)

time: 40 us -> 39.7 us (level)
  no operation moved by 1% of the time
where the time goes in v4:
time: 39.7 us; the launch traced here: 39.6 us
  Pallas kernels  38.9 us (98%)
  between operations  0.65 us (2%)
    pallas_call x1, Pallas kernels, on_device(): pl.pallas_call(kernel, out_shape=[pltpu.VMEM(shape.shape, F32) for shape...  37.5 us
    pallas_call x1, Pallas kernels, on_device(): pl.pallas_call(finish, out_shape=out_shape, in_specs=[vmem_spec] * 8, out...  1.45 us

profile of v4, /device:TPU:1, one launch (start us, length us, event | category | flops | bytes accessed | tf_op | source)
XLA Modules:
  0.0 39.6 jit_solution(11754520678616658467)
XLA Ops:
  0.6 37.5 %shard_map.206 = (f32[4,192]{1,0:T(4,128)S(1)}, f32[4,144]{1,0:T(4,128)S(1)}, f32[4,192]{1,0:T(4,128)S(1)}, f32[4,144]{1,0:T(4,128)S(1)}, f32[4,192]{1,0:T(4,128...) custom-call(bf16[4,192]{1,0:T(4,128)(2,1)} %q_in.1, bf16[4,144]{1,0:T(4,128)(2,1)} %qp_in.1, ...), custom_call_target="tpu_custom_call" | custom-call | flops 1000000000 | bytes 5242880 | tf_op jit(solution)/shard_map/pallas_call | solution.py:586
  38.1 1.5 %shard_map.207 = (f32[4,192]{1,0:T(4,128)}, f32[4,144]{1,0:T(4,128)}, f32[4,192]{1,0:T(4,128)}, f32[4,144]{1,0:T(4,128)}, f32[4,192]{1,0:T(4,128)}, /*index=5*/f...) custom-call(f32[4,192]{1,0:T(4,128)S(1)} %get-tuple-element.24.refs_0_, f32[4,144]{1,0:T(4,128)S(1)} %get-tuple-element.25.refs_1_, ...), custom_call_target="tpu_custom_call" | custom-call | tf_op jit(solution)/shard_map/pallas_call | solution.py:601

commit v5 on v4

--- a/solution.py
+++ b/solution.py
@@ -16,7 +16,6 @@
 TILE = 64
 PEERS = 16
 VMEM_LIMIT = 40 * 2**20
-PIECES = 8
 W_LOGIT = math.sqrt(1.0 / 3.0)
 W_POINT = math.sqrt(2.0 / 36.0)
 SCALE_Q = W_LOGIT / 4.0
@@ -332,6 +331,12 @@
         stats[0] = acc_m
         stats[1] = acc_s
 
+    row_max, row_sum = stats[0], stats[1]
+    any_live = row_sum > 0
+    safe = jnp.where(any_live, row_sum, 1.0)
+    lse = jnp.where(any_live, row_max + jnp.log(safe), NEG_FILL)
+    inverse = 1.0 / safe
+
     wait_recv(gzg, 2)
 
     gz12[...] = gzg[...].astype(F32).reshape(PEERS * 4 * H, 128)
@@ -358,11 +363,7 @@
         acc = jnp.where(lane_pair == p, sums[HP * p : HP * p + HP], acc)
     stats[2] = acc
 
-    row_max, row_sum = stats[0], stats[1]
-    any_live = row_sum > 0
-    safe = jnp.where(any_live, row_sum, 1.0)
-    lse = jnp.where(any_live, row_max + jnp.log(safe), NEG_FILL)
-    mean = jnp.where(any_live, stats[2] / safe, 0.0)
+    mean = jnp.where(any_live, stats[2] * inverse, 0.0)
     stat_send[...] = jnp.where(left, lse, pltpu.roll(mean, 64, 1))
     stat_g[c] = stat_send[...]
     spread(stat_send, stat_g, "col", 3)
@@ -539,9 +540,7 @@
 
 def finish(*refs):
     sem = refs[-1]
-    rows = 4096 // PIECES
-    pairs = [(refs[6].at[pl.ds(rows * n, rows)], refs[14].at[pl.ds(rows * n, rows)]) for n in range(PIECES)]
-    pairs += [(refs[n], refs[8 + n]) for n in range(8) if n != 6]
+    pairs = [(refs[n], refs[8 + n]) for n in (6, 0, 1, 2, 3, 4, 5, 7)]
     copies = [pltpu.make_async_copy(src, dst, sem.at[n]) for n, (src, dst) in enumerate(pairs)]
     for copy in copies:
         copy.start()
@@ -603,7 +602,7 @@
         out_shape=out_shape,
         in_specs=[vmem_spec] * 8,
         out_specs=[any_spec] * 8,
-        scratch_shapes=[pltpu.SemaphoreType.DMA((7 + PIECES,))],
+        scratch_shapes=[pltpu.SemaphoreType.DMA((8,))],
         compiler_params=pltpu.CompilerParams(vmem_limit_bytes=2**20),
     )(*out)
     return (*out[:6], out[6].reshape(TILE, TILE, 128), out[7].T)

time: 39.7 us -> 39.6 us (level)
  no operation moved by 1% of the time
where the time goes in v5:
time: 39.6 us; the launch traced here: 39.5 us
  Pallas kernels  38.9 us (98%)
  between operations  0.65 us (2%)
    pallas_call x1, Pallas kernels, on_device(): pl.pallas_call(kernel, out_shape=[pltpu.VMEM(shape.shape, F32) for shape...  37.5 us
    pallas_call x1, Pallas kernels, on_device(): pl.pallas_call(finish, out_shape=out_shape, in_specs=[vmem_spec] * 8, out...  1.41 us

profile of v5, /device:TPU:1, one launch (start us, length us, event | category | flops | bytes accessed | tf_op | source)
XLA Modules:
  0.0 39.5 jit_solution(4549297464513212097)
XLA Ops:
  0.6 37.5 %shard_map.206 = (f32[4,192]{1,0:T(4,128)S(1)}, f32[4,144]{1,0:T(4,128)S(1)}, f32[4,192]{1,0:T(4,128)S(1)}, f32[4,144]{1,0:T(4,128)S(1)}, f32[4,192]{1,0:T(4,128...) custom-call(bf16[4,192]{1,0:T(4,128)(2,1)} %q_in.1, bf16[4,144]{1,0:T(4,128)(2,1)} %qp_in.1, ...), custom_call_target="tpu_custom_call" | custom-call | flops 1000000000 | bytes 5242880 | tf_op jit(solution)/shard_map/pallas_call | solution.py:585
  38.1 1.4 %shard_map.207 = (f32[4,192]{1,0:T(4,128)}, f32[4,144]{1,0:T(4,128)}, f32[4,192]{1,0:T(4,128)}, f32[4,144]{1,0:T(4,128)}, f32[4,192]{1,0:T(4,128)}, /*index=5*/f...) custom-call(f32[4,192]{1,0:T(4,128)S(1)} %get-tuple-element.24.refs_0_, f32[4,144]{1,0:T(4,128)S(1)} %get-tuple-element.25.refs_1_, ...), custom_call_target="tpu_custom_call" | custom-call | tf_op jit(solution)/shard_map/pallas_call | solution.py:600
